TPU v7x, 256 devices: a whole 4x4x8 slice. The times are simulated.
256 devices in a mesh: crop: 8 (over z_lo, y), dap: 32 (over z_hi, x, core).
Axes of the slice: x: 4, y: 4, z: 8 (z_hi: 4, z_lo: 2; z = z_hi * 2 + z_lo), core: 2. Of those that a mesh axis runs over, the one named last changes fastest.
Arguments:
- alignment: bfloat16 [512, 512, 256], P(('crop', 'dap')), parts along dimension 0, may hold values from -6 to 6
- alignment_mask: int32 [512, 512], P('crop'), parts along dimension 0, may hold values from 0 to 1, as said below
- cotangent: bfloat16 [4096, 512, 128], P(('crop', 'dap')), parts along dimension 0, may hold values from -6 to 6
- scales: float32 [256], replicated, may hold values from 0.1 to 1.9
- shifts: float32 [256], replicated, may hold values from -3 to 3
- projection: bfloat16 [256, 64], replicated, may hold values from -0.375 to 0.375
- offsets: float32 [64], replicated, may hold values from -3 to 3
- readout: bfloat16 [1024, 128], replicated, may hold values from -0.1875 to 0.1875
- biases: float32 [128], replicated, may hold values from -12 to 12
Outputs:
- pair_update: bfloat16 [4096, 512, 128], P(('crop', 'dap')), parts along dimension 0
- alignment_grad: bfloat16 [512, 512, 256], P(('crop', 'dap')), parts along dimension 0
- projection_grad: float32 [2048, 64], P('crop'), parts along dimension 0
- offsets_grad: float32 [512], P('crop'), parts along dimension 0
- readout_grad: float32 [8192, 128], P('crop'), parts along dimension 0
- biases_grad: float32 [1024], P('crop'), parts along dimension 0
- scales_grad: float32 [2048], P('crop'), parts along dimension 0
- shifts_grad: float32 [2048], P('crop'), parts along dimension 0
There are 8 independent parts, one for each index of `crop`. A program takes and returns all parts, laid end to end along the dimension named above; an argument that names none is the same for every part. Nothing has to cross between parts.
Inputs may be any that keep to these rules, and one draw needn't show every extreme that they name: `alignment_mask`: sequence 0 is 1 at every residue.
All inputs are finite; a program needn't handle non-finite values.
Results may differ from a plain program's by a relative error of at most 0.03.
Values may be sent and summed in bfloat16 or wider, within the bound.
A program may use at most 128 MiB of HBM per device.

v0:
```python
import math

import jax
import jax.numpy as jnp
from jax import lax
from jax.sharding import PartitionSpec as P


def layer_stats(values, scales, shifts):
    wide = values.astype(jnp.float32)
    center = jnp.mean(wide, axis=-1, keepdims=True)
    spread = jnp.mean(jnp.square(wide - center), axis=-1, keepdims=True)
    inverse = lax.rsqrt(spread + 1e-05)
    standard = (wide - center) * inverse
    normed = (standard * scales + shifts).astype(jnp.bfloat16)
    return (standard, inverse, normed)


def side_values(normed, projection, offsets, mask_part):
    projected = (
        jnp.einsum("snm,mk->snk", normed, projection, preferred_element_type=jnp.float32) + offsets
    )
    return (projected * mask_part[:, :, None]).astype(jnp.bfloat16)


def local_grads(proj_grad, normed, standard, inverse, projection, scales):
    normed_grad = jnp.einsum(
        "snk,mk->snm", proj_grad, projection, preferred_element_type=jnp.float32
    )
    scales_part = jnp.sum(normed_grad * standard, axis=(0, 1))
    shifts_part = jnp.sum(normed_grad, axis=(0, 1))
    projection_part = jnp.einsum(
        "snm,snk->mk", normed, proj_grad, preferred_element_type=jnp.float32
    )
    offsets_part = jnp.sum(proj_grad.astype(jnp.float32), axis=(0, 1))
    hatted = normed_grad * scales
    values_grad = (
        hatted
        - jnp.mean(hatted, axis=-1, keepdims=True)
        - standard * jnp.mean(hatted * standard, axis=-1, keepdims=True)
    ) * inverse
    return (
        values_grad.astype(jnp.bfloat16),
        projection_part,
        offsets_part,
        scales_part,
        shifts_part,
    )


def per_device(
    alignment, alignment_mask, cotangent, scales, shifts, projection, offsets, readout, biases
):
    groups = lax.axis_size("dap")
    position = lax.axis_index("dap")
    residues = alignment.shape[1]
    res_local = residues // groups
    channels = projection.shape[1] // 2
    mask_all = alignment_mask.astype(jnp.float32)
    mask_own = lax.dynamic_slice_in_dim(mask_all, position * res_local, res_local, 1)
    columns = lax.all_to_all(alignment, "dap", split_axis=1, concat_axis=0, tiled=True)
    standard, inverse, normed = layer_stats(columns, scales, shifts)
    both_sides = side_values(normed, projection, offsets, mask_own)
    left_side = both_sides[:, :, :channels]
    right_side = both_sides[:, :, channels:]
    sequences = left_side.shape[0]
    right_rows = jnp.transpose(right_side, (1, 0, 2)).reshape(res_local, sequences * channels)
    right_all = lax.all_gather(right_rows, "dap", axis=0, tiled=True).reshape(
        residues, sequences, channels
    )
    intersection = jnp.dot(mask_own.T, mask_all, precision=lax.Precision.HIGHEST)
    divisor = 0.001 + intersection
    scaled_grad = (cotangent.astype(jnp.float32) / divisor[:, :, None]).astype(jnp.bfloat16)
    biases_part = jnp.sum(scaled_grad.astype(jnp.float32), axis=(0, 1))
    stride = math.gcd(residues, 128)

    def step_fn(carried, column_at):
        readout_acc, left_acc = carried
        right_piece = lax.dynamic_slice_in_dim(right_all, column_at, stride, 0)
        divisor_piece = lax.dynamic_slice_in_dim(divisor, column_at, stride, 1)
        grad_piece = lax.dynamic_slice_in_dim(scaled_grad, column_at, stride, 1)
        products = jnp.einsum(
            "sic,jsd->ijcd", left_side, right_piece, preferred_element_type=jnp.float32
        )
        products = products.reshape(res_local, stride, channels * channels).astype(jnp.bfloat16)
        mixed = (
            jnp.einsum("ijk,kz->ijz", products, readout, preferred_element_type=jnp.float32)
            + biases
        )
        update = (mixed / divisor_piece[:, :, None]).astype(jnp.bfloat16)
        readout_acc = readout_acc + jnp.einsum(
            "ijk,ijz->kz", products, grad_piece, preferred_element_type=jnp.float32
        )
        products_grad = jnp.einsum(
            "ijz,kz->ijk", grad_piece, readout, preferred_element_type=jnp.float32
        )
        products_grad = products_grad.astype(jnp.bfloat16).reshape(
            res_local, stride, channels, channels
        )
        left_acc = left_acc + jnp.einsum(
            "ijcd,jsd->sic", products_grad, right_piece, preferred_element_type=jnp.float32
        )
        partial_terms = jnp.einsum(
            "ijcd,sic->jsd", products_grad, left_side, preferred_element_type=jnp.float32
        )
        return (
            (readout_acc, left_acc),
            (update, partial_terms.reshape(stride, sequences * channels)),
        )

    column_starts = jnp.arange(residues // stride, dtype=jnp.int32) * stride
    initial = (
        jnp.zeros((channels * channels, readout.shape[1]), jnp.float32),
        jnp.zeros((sequences, res_local, channels), jnp.float32),
    )
    (readout_part, left_grad), stacked = lax.scan(step_fn, initial, column_starts)
    updates, partial_all = stacked
    right_grad = lax.psum_scatter(
        partial_all.reshape(residues, sequences * channels).astype(jnp.bfloat16),
        "dap",
        scatter_dimension=0,
        tiled=True,
    ).astype(jnp.float32)
    pair_update = jnp.transpose(updates, (1, 0, 2, 3)).reshape(
        res_local, residues, readout.shape[1]
    )
    right_local = jnp.transpose(right_grad.reshape(res_local, sequences, channels), (1, 0, 2))
    proj_grad = (jnp.concatenate([left_grad, right_local], axis=-1) * mask_own[:, :, None]).astype(
        jnp.bfloat16
    )
    column_values, projection_part, offsets_part, scales_part, shifts_part = local_grads(
        proj_grad, normed, standard, inverse, projection, scales
    )
    alignment_grad = lax.all_to_all(column_values, "dap", split_axis=0, concat_axis=1, tiled=True)
    totals = (
        lax.psum(projection_part.astype(jnp.bfloat16), "dap").astype(jnp.float32),
        lax.psum(offsets_part.astype(jnp.bfloat16), "dap").astype(jnp.float32),
        lax.psum(readout_part.astype(jnp.bfloat16), "dap").astype(jnp.float32),
        lax.psum(biases_part.astype(jnp.bfloat16), "dap").astype(jnp.float32),
        lax.psum(scales_part.astype(jnp.bfloat16), "dap").astype(jnp.float32),
        lax.psum(shifts_part.astype(jnp.bfloat16), "dap").astype(jnp.float32),
    )
    return (
        pair_update,
        alignment_grad,
        totals[0],
        totals[1],
        totals[2],
        totals[3],
        totals[4],
        totals[5],
    )


def solution(mesh):
    return jax.shard_map(
        per_device,
        mesh=mesh,
        in_specs=(
            P(("crop", "dap"), None, None),
            P("crop", None),
            P(("crop", "dap"), None, None),
            P(),
            P(),
            P(),
            P(),
            P(),
            P(),
        ),
        out_specs=(
            P(("crop", "dap"), None, None),
            P(("crop", "dap"), None, None),
            P("crop", None),
            P("crop"),
            P("crop", None),
            P("crop"),
            P("crop"),
            P("crop"),
        ),
        check_vma=False,
    )
```

profile of v0, /device:TPU:1, one launch (start us, length us, event | category | flops | bytes accessed | tf_op | source)
XLA Modules:
  0.0 780.4 jit_solution(4863911275570852756)
XLA Ops:
  7.2 2.4 copy.66
  9.6 12.6 %all-to-all-start = ((bf16[2,512,256]{2,0,1:T(2,128)(2,1)}), bf16[2,512,256]{2,0,1:T(2,128)(2,1)S(1)}, u32[]{:S(2)}, u32[]{:S(2)}) async-start(bf16[2,512,256]{2,0,1:T(2,128)(2,1)} %copy.66), calls=%async_computation | async-start | bytes 1048576 | tf_op jit(solution)/shard_map/all_to_all | solution.py:61
  22.4 17.9 %all-to-all-done = bf16[2,512,256]{2,0,1:T(2,128)(2,1)S(1)} async-done(((bf16[2,512,256]{2,0,1:T(2,128)(2,1)}), bf16[2,512,256]{2,0,1:T(2,128)(2,1)S(1)}, u32[]{:S(2)}, u32[]{:S(2)}) %all-to-all-start) | async-done | bytes 524320 | tf_op jit(solution)/shard_map/all_to_all | solution.py:61
  45.3 3.2 fusion.41
  49.4 46.3 %all-gather.2.cloned.1.call-done = bf16[512,2048]{1,0:T(8,128)(2,1)} async-done(((bf16[16,2048]{1,0:T(8,128)(2,1)}), bf16[512,2048]{1,0:T(8,128)(2,1)}) %all-gather.2.cloned.1.call-update) | async-done | bytes 2097168 | tf_op jit(solution)/shard_map/all_gather | solution.py:68
  95.6 3.9 copy.69
  99.5 144.4 %while.17 = (s32[]{:T(128)}, f32[1024,128]{1,0:T(8,128)}, f32[64,16,32]{0,2,1:T(8,128)}, bf16[4,16,128,128]{3,2,1,0:T(8,128)(2,1)}, bf16[4,128,2048]{2,1,0:T(8,1...) while((s32[]{:T(128)}, f32[1024,128]{1,0:T(8,128)}, ...), condition=%wide.region_3.4_spmd.clone, body=%wide.region_2.0_spmd.clone.sunk | while | flops 2421227520 | bytes 84829960 | solution.py:116
  104.2 2.1 convert_bitcast_fusion.2
  106.3 2.7 copy.124
  109.1 1.8 copy-done.1
  111.0 2.3 fusion.80
  113.3 4.3 fusion.78
  117.5 3.2 convolution_convert_fusion.2
  120.7 6.4 copy.125
  127.1 4.7 fusion.79
  131.8 2.4 fusion.81
  140.2 2.1 convert_bitcast_fusion.2
  142.4 2.7 copy.124
  145.2 1.8 copy-done.1
  147.0 2.3 fusion.80
  149.3 4.4 fusion.78
  153.7 3.2 convolution_convert_fusion.2
  156.9 6.4 copy.125
  163.3 4.7 fusion.79
  168.0 2.4 fusion.81
  176.4 2.1 convert_bitcast_fusion.2
  178.6 2.7 copy.124
  181.4 1.8 copy-done.1
  183.2 2.3 fusion.80
  185.5 4.4 fusion.78
  189.9 3.2 convolution_convert_fusion.2
  193.0 6.4 copy.125
  199.5 4.7 fusion.79
  204.2 2.4 fusion.81
  212.4 2.1 convert_bitcast_fusion.2
  214.6 2.7 copy.124
  217.4 1.8 copy-done.1
  219.2 2.3 fusion.80
  221.5 4.4 fusion.78
  225.8 3.2 convolution_convert_fusion.2
  229.0 6.4 copy.125
  235.5 4.7 fusion.79
  240.2 2.4 fusion.81
  245.3 85.0 %reduce-scatter.2.cloned.1.call-done = bf16[16,2048]{1,0:T(8,128)(2,1)} async-done(((bf16[512,2048]{1,0:T(8,128)(2,1)}), bf16[16,2048]{1,0:T(8,128)(2,1)}) %reduce-scatter.2.cloned.1.call-update) | async-done | bytes 65552 | tf_op jit(solution)/shard_map/reduce_scatter | solution.py:118
  334.3 8.5 %all-to-all-start.1 = ((bf16[64,16,256]{2,1,0:T(8,128)(2,1)}), bf16[64,16,256]{2,1,0:T(8,128)(2,1)S(1)}, u32[]{:S(2)}, u32[]{:S(2)}) async-start(bf16[64,16,256]{2,1,0:T(8,128)(2,1)} %multiply_convert_fusion), calls=%async_computation.2 | async-start | bytes 1048576 | tf_op jit(solution)/shard_map/all_to_all | solution.py:134
  344.7 3.2 copy.72
  347.9 282.2 %all-reduce.3.cloned.1.call-done = bf16[1024,128]{1,0:T(8,128)(2,1)} async-done(((bf16[1024,128]{1,0:T(8,128)(2,1)}), bf16[1024,128]{1,0:T(8,128)(2,1)}) %all-reduce.3.cloned.1.call-update) | async-done | bytes 262160 | tf_op jit(solution)/shard_map/psum | solution.py:138
  632.1 138.1 %all-reduce = (bf16[256,64]{0,1:T(8,128)(2,1)S(1)}, bf16[64]{0:T(256)(128)(2,1)S(1)}, bf16[128]{0:T(256)(128)(2,1)S(1)}, bf16[256]{0:T(256)(128)(2,1)S(1)}, bf16[256]{0:T(256)(128)(2,1)S(1)}) all-reduce(bf16[256,64]{0,1:T(8,128)(2,1)S(1)} %fusion.32, ...), channel_id=1, replica_groups=mesh['crop'=8,'dap'=32] {'dap'}, use_global_device_ids=true, to_apply=%region_7.8 | all-reduce | flops 17088 | bytes 68352 | tf_op jit(solution)/shard_map/psum | solution.py:136
  (105 shorter events, 35.2 us)
Async XLA Ops:
  7.2 35.8 %copy-start = (bf16[256,64]{0,1:T(8,128)(2,1)S(1)}, bf16[256,64]{0,1:T(8,128)(2,1)}, u32[]{:S(2)}) copy-start(bf16[256,64]{0,1:T(8,128)(2,1)} %param.16) | copy-start | bytes 98308
  7.2 15.1 %copy-start.8 = (s32[64,512]{1,0:T(8,128)S(1)}, s32[64,512]{1,0:T(8,128)}, u32[]{:S(2)}) copy-start(s32[64,512]{1,0:T(8,128)} %param.12) | copy-start | bytes 393220
  9.6 30.6 %all-to-all-start = ((bf16[2,512,256]{2,0,1:T(2,128)(2,1)}), bf16[2,512,256]{2,0,1:T(2,128)(2,1)S(1)}, u32[]{:S(2)}, u32[]{:S(2)}) async-start(bf16[2,512,256]{2,0,1:T(2,128)(2,1)} %copy.66), calls=%async_computation | async-start | bytes 1048576 | tf_op jit(solution)/shard_map/all_to_all | solution.py:61
  22.2 73.4 %all-gather.2.cloned.1.call-start = ((), (), s32[]{:S(2)}) async-start(), calls=%async_computation.3 | async-start | bytes 2162688 | tf_op jit(solution)/shard_map/all_gather | solution.py:68
  41.4 1.6 copy-start.11
  41.4 1.5 copy-start.12
  41.4 1.5 copy-start.13
  41.5 1.8 copy-start.9
  41.6 1.8 copy-start.5
  42.0 1.0 copy-start.3
  44.4 285.8 %reduce-scatter.2.cloned.1.call-start = ((), (), s32[]{:S(2)}) async-start(), calls=%async_computation.4 | async-start | bytes 2162688 | tf_op jit(solution)/shard_map/reduce_scatter | solution.py:118
  49.4 50.2 %copy-start.7 = (bf16[1024,128]{1,0:T(8,128)(2,1)S(1)}, bf16[1024,128]{1,0:T(8,128)(2,1)}, u32[]{:S(2)}) copy-start(bf16[1024,128]{1,0:T(8,128)(2,1)} %param.18) | copy-start | bytes 786436
  49.4 50.2 %copy-start.14 = (f32[128]{0:T(128)S(1)}, f32[128]{0:T(128)}, u32[]{:S(2)}) copy-start(f32[128]{0:T(128)} %param.19) | copy-start | bytes 1540
  109.0 1.9 copy-start.1
  127.1 4.7 copy-start.2
  145.1 1.9 copy-start.1
  163.3 4.7 copy-start.2
  181.3 1.9 copy-start.1
  199.5 4.7 copy-start.2
  217.3 1.9 copy-start.1
  235.5 4.7 copy-start.2
  244.0 88.0 %copy-start.4 = (f32[64,16,256]{2,1,0:T(8,128)S(1)}, f32[64,16,256]{2,1,0:T(8,128)}, u32[]{:S(2)}) copy-start(f32[64,16,256]{2,1,0:T(8,128)} %copy-done.3) | copy-start | bytes 3145732
  331.6 1.2 copy-start.6
  331.6 1.2 copy-start.10
  334.3 438.7 %all-to-all-start.1 = ((bf16[64,16,256]{2,1,0:T(8,128)(2,1)}), bf16[64,16,256]{2,1,0:T(8,128)(2,1)S(1)}, u32[]{:S(2)}, u32[]{:S(2)}) async-start(bf16[64,16,256]{2,1,0:T(8,128)(2,1)} %multiply_convert_fusion), calls=%async_computation.2 | async-start | bytes 1048576 | tf_op jit(solution)/shard_map/all_to_all | solution.py:134
  342.9 287.3 %all-reduce.3.cloned.1.call-start = ((), (), s32[]{:S(2)}) async-start(), calls=%async_computation.5 | async-start | bytes 524288 | tf_op jit(solution)/shard_map/psum | solution.py:138
Sparse Core Ops, SparseCore 0:
  44.6 51.0 all-gather.1
  244.1 86.1 reduce-scatter.1
  346.3 283.7 all-reduce.2
where the time goes:
time: 787 us; the launch traced here: 780 us
  waiting for transfers between devices  431 us (55%)
  blocking collectives  138 us (18%)
  matrix products  77.4 us (10%)
  local copies, waits for them, and re-layouts  76.8 us (10%)
  starting transfers between devices  21.2 us (3%)
  between operations  14.1 us (2%)
  other arithmetic  13.4 us (2%)
  loops' own time  7.96 us (1%)
    psum x1, waiting for transfers between devices, per_device(): lax.psum(readout_part.astype(jnp.bfloat16), 'dap').astype(jnp.float32)  282 us
    psum x1, blocking collectives, per_device(): lax.psum(projection_part.astype(jnp.bfloat16), 'dap').astype(jnp.float32)  138 us
    reduce_scatter x1, waiting for transfers between devices, per_device(): lax.psum_scatter(partial_all.reshape(residues, sequences * channels).asty...  85 us
    all_gather x1, waiting for transfers between devices, per_device(): lax.all_gather(right_rows, 'dap', axis=0, tiled=True)  46.3 us
    convert_element_type x4, local copies, waits for them, and re-layouts, step_fn(): products_grad.astype(jnp.bfloat16)  25.7 us
    dot_general x4, matrix products, step_fn(): jnp.einsum('ijcd,jsd->sic', products_grad, right_piece, preferred_element...  18.9 us
    all_to_all x1, waiting for transfers between devices, per_device(): lax.all_to_all(alignment, 'dap', split_axis=1, concat_axis=0, tiled=True)  17.9 us
    dot_general x4, matrix products, step_fn(): jnp.einsum('ijk,ijz->kz', products, grad_piece, preferred_element_type=jn...  17.3 us
  transfers between devices with their start and end apart: 5, of which 4 were waited for; matrix products, arithmetic and copies ran while one was open for 2% of the time, Pallas kernels for 0%

commit v1 on v0

v1 whole, which is shorter than its diff:
```python
import jax
import jax.numpy as jnp
from jax import lax
from jax.experimental import pallas as pl
from jax.experimental.pallas import tpu as pltpu
from jax.sharding import PartitionSpec as P

F32 = jnp.float32
BF16 = jnp.bfloat16
MESH = pl.DeviceIdType.MESH


def mm(a, b):
    return lax.dot_general(a, b, (((1,), (0,)), ((), ())), preferred_element_type=F32)


def mm_nt(a, b):
    return lax.dot_general(a, b, (((1,), (1,)), ((), ())), preferred_element_type=F32)


def mm_tn(a, b):
    return lax.dot_general(a, b, (((0,), (0,)), ((), ())), preferred_element_type=F32)


def iota(shape, dim):
    return lax.broadcasted_iota(jnp.int32, shape, dim)


def kernel(
    al, mask, cot, scales, shifts, proj, offs, readout, biases,
    pair_o, al_o, pg_o, og_o, rg_o, bg_o, sg_o, hg_o,
    mcol, std, inv, normed, both, l_out, l_in, l_f, l_all, l_t, w, ro_f,
    rec, g, perm, perm_t, r_buf, r_k, r_j, t, q,
    d_buf, c_in, s1, x_in, s2, z_in,
    lg_f, lg_out, lg_in, rg_l, rg_f, rg_b, ra, rb, rc_send, rc, rh, rk,
    pb, pb_core, pb_x, pb_xs, pb_z, pb_half, pb_other, bsum,
    l_ss, l_rs, e_ss, e_rs, r_ss, r_rs, d_ss, d_rs, a_ss, a_rs, b_ss, b_rs,
):
    me = lax.axis_index("dap")
    core = lax.rem(me, 2)
    xx = lax.rem(lax.div(me, 2), 4)
    zz = lax.div(me, 8)
    sign = 1 - 2 * core
    xs, xm, xf = (lax.rem(xx + 4 + sign, 4), lax.rem(xx + 4 - sign, 4), lax.rem(xx + 2, 4))
    zs, zm, zf = (lax.rem(zz + 4 + sign, 4), lax.rem(zz + 4 - sign, 4), lax.rem(zz + 2, 4))
    other = 1 - core

    def dev(z, x, c):
        return (z * 4 + x) * 2 + c

    def slot(x, c, z):
        return (x * 2 + c) * 4 + z

    def slot_dev(s):
        return dev(lax.rem(s, 4), lax.div(s, 8), lax.rem(lax.div(s, 4), 2))

    sib = dev(zz, xx, other)
    mine = slot(xx, core, zz)

    def remote(src, dst, ss, rs, target):
        return pltpu.make_async_remote_copy(
            src_ref=src, dst_ref=dst, send_sem=ss, recv_sem=rs,
            device_id={"dap": target}, device_id_type=MESH,
        )

    barrier = pltpu.get_barrier_semaphore()

    def greet(k, carry):
        pl.semaphore_signal(
            barrier, inc=1, device_id={"dap": lax.rem(me + k, 32)}, device_id_type=MESH
        )
        return carry

    lax.fori_loop(1, 32, greet, 0)

    mask_f = mask[...].astype(F32)
    mask_t = mask_f.T
    for k in range(2):
        mcol[k * 512:(k + 1) * 512, :] = jnp.sum(
            jnp.where(iota((512, 64), 1) == 2 * me + k, mask_t, 0.0), axis=1, keepdims=True
        )

    def norm_step(b, carry):
        rows = pl.ds(pl.multiple_of(b * 128, 128), 128)
        wide = al[rows, :].astype(F32)
        center = jnp.mean(wide, axis=-1, keepdims=True)
        dev_ = wide - center
        spread = jnp.mean(dev_ * dev_, axis=-1, keepdims=True)
        inverse = lax.rsqrt(spread + 1e-05)
        standard = dev_ * inverse
        std[rows, :] = standard
        inv[rows, :] = inverse
        nb = (standard * scales[...] + shifts[...]).astype(BF16)
        normed[rows, :] = nb
        sides = (mm(nb, proj[...]) + offs[...]) * mcol[rows, :]
        both[rows, :] = sides
        return carry

    lax.fori_loop(0, 8, norm_step, 0)
    cat = jnp.concatenate([both[0:512, :], both[512:1024, :]], axis=1)
    l_out[...] = cat.astype(BF16).reshape(32, 16, 128)
    cat_t = cat.T
    r_buf[mine] = jnp.concatenate([cat_t[32:64], cat_t[96:128]], axis=0).astype(BF16)

    pl.semaphore_wait(barrier, 31)

    def r_send(s, target, k):
        remote(r_buf.at[s], r_buf.at[s], r_ss.at[k], r_rs.at[s], target).start()

    def r_wait(s):
        remote(r_buf.at[s], r_buf.at[s], r_ss.at[0], r_rs.at[s], sib).wait_recv()

    r_send(mine, dev(zs, xx, core), 0)
    r_send(mine, dev(zm, xx, core), 1)
    r_send(mine, dev(zz, xs, core), 2)
    r_send(mine, dev(zz, xm, core), 3)
    r_send(mine, sib, 4)

    def l_copy(k):
        s = lax.rem(mine + k, 32)
        p = slot_dev(s)
        return remote(l_out.at[p], l_in.at[mine], l_ss.at[k], l_rs.at[mine], p)

    def l_send(k, carry):
        l_copy(k).start()
        return carry

    lax.fori_loop(1, 32, l_send, 0)
    l_in[mine] = l_out[me]

    mask_b = mask_f.astype(BF16)
    own_cols = (iota((512, 16), 0) == 16 * me + iota((512, 16), 1)).astype(F32).astype(BF16)
    mask_own = mm(mask_b, own_cols).astype(BF16)
    recip = 1.0 / (0.001 + mm(mask_t.astype(BF16), mask_own))
    total = jnp.zeros((1, 128), F32)
    for i in range(16):
        rec_i = jnp.broadcast_to(recip[:, i:i + 1], (512, 128))
        rec[i] = rec_i
        sg = (cot[i].astype(F32) * rec_i).astype(BF16)
        g[:, i * 128:(i + 1) * 128] = sg
        total = total + jnp.sum(sg.astype(F32), axis=0, keepdims=True)
    bsum[...] = total

    ro_f[...] = readout[...].astype(F32)
    for d in range(32):
        w[:, d * 128:(d + 1) * 128] = ro_f[pl.ds(d, 32, stride=32), :].astype(BF16)

    def packed(a):
        return lax.rem(a, 8) * 64 + lax.rem(lax.div(a, 8), 2) * 32 + lax.div(a, 16)

    perm[...] = (iota((512, 512), 1) == packed(iota((512, 512), 0))).astype(F32).astype(BF16)
    perm_t[...] = (iota((512, 512), 0) == packed(iota((512, 512), 1))).astype(F32).astype(BF16)

    def l_wait(k, carry):
        s = lax.rem(mine + k, 32)
        remote(l_out.at[0], l_in.at[s], l_ss.at[k], l_rs.at[s], sib).wait_recv()
        return carry

    lax.fori_loop(1, 32, l_wait, 0)
    l_f[...] = l_in[...].reshape(512, 128).astype(F32)
    for i in range(16):
        v = l_f[pl.ds(i, 32, stride=16), :]
        parts = [v[x * 8:x * 8 + 8, k * 64:k * 64 + 32] for x in range(4) for k in range(2)]
        l_all[i * 64:(i + 1) * 64, :] = jnp.concatenate(parts, axis=0).astype(BF16)
    l_t[...] = l_all[...].astype(F32).T.astype(BF16)

    def t_step(dp, carry):
        wb = w[:, pl.ds(pl.multiple_of(dp * 256, 256), 256)]
        r = mm(l_all[...], wb).astype(BF16)
        for i in range(16):
            for dd in range(2):
                t[:, 2 * dp + dd, :, i * 128:(i + 1) * 128] = r[
                    i * 64:(i + 1) * 64, dd * 128:(dd + 1) * 128
                ].reshape(4, 16, 128)
        return carry

    lax.fori_loop(0, 16, t_step, 0)

    r_wait(slot(xx, core, zm))
    r_send(slot(xx, core, zm), dev(zs, xx, core), 5)
    for n, z_ in enumerate((zm, zs)):
        if n == 1:
            r_wait(slot(xx, core, z_))
        r_send(slot(xx, core, z_), dev(zz, xs, core), 6 + 3 * n)
        r_send(slot(xx, core, z_), dev(zz, xm, core), 7 + 3 * n)
        r_send(slot(xx, core, z_), sib, 8 + 3 * n)

    def d_group(x_, n):
        raw = mm_nt(t[x_].reshape(512, 2048), g[...]).astype(BF16)
        d_buf[x_] = mm(perm_t[...], raw).astype(BF16).reshape(2, 256, 512)
        remote(
            d_buf.at[x_, other], c_in.at[x_], d_ss.at[n], d_rs.at[x_], sib
        ).start()

    d_group(xf, 0)
    r_wait(slot(xx, core, zf))
    r_send(slot(xx, core, zf), dev(zz, xs, core), 12)
    r_send(slot(xx, core, zf), dev(zz, xm, core), 13)
    r_send(slot(xx, core, zf), sib, 14)
    r_wait(slot(xm, core, zz))
    r_send(slot(xm, core, zz), dev(zz, xs, core), 15)
    r_send(slot(xm, core, zz), sib, 16)
    r_wait(slot(xs, core, zz))
    r_send(slot(xs, core, zz), sib, 17)
    d_group(xm, 1)
    for n, z_ in enumerate((zm, zs)):
        r_wait(slot(xm, core, z_))
        r_send(slot(xm, core, z_), dev(zz, xs, core), 18 + 3 * n)
        r_send(slot(xm, core, z_), sib, 19 + 3 * n)
        r_wait(slot(xs, core, z_))
        r_send(slot(xs, core, z_), sib, 20 + 3 * n)
    d_group(xs, 2)
    r_wait(slot(xm, core, zf))
    r_send(slot(xm, core, zf), dev(zz, xs, core), 24)
    r_send(slot(xm, core, zf), sib, 25)
    r_wait(slot(xs, core, zf))
    r_send(slot(xs, core, zf), sib, 26)
    r_wait(slot(xf, core, zz))
    r_send(slot(xf, core, zz), sib, 27)
    d_group(xx, 3)

    def wide(ref):
        return ref[...].astype(F32)

    def c_wait(x_, n):
        remote(d_buf.at[x_, other], c_in.at[x_], d_ss.at[n], d_rs.at[x_], sib).wait_recv()

    def core_sum(x_):
        return d_buf[x_, core].astype(F32) + c_in[x_].astype(F32)

    def x_copy(x_, n, target_x):
        return remote(
            s1.at[x_], x_in.at[n], d_ss.at[4 + n], d_rs.at[4 + n], dev(zz, target_x, core)
        )

    c_wait(xf, 0)
    s1[xf] = core_sum(xf).astype(BF16)
    x_copy(xf, 0, xs).start()
    c_wait(xm, 1)
    s1[xm] = core_sum(xm).astype(BF16)
    x_copy(xm, 1, xm).start()

    for n, z_ in enumerate((zm, zs, zf)):
        r_wait(slot(xf, core, z_))
        r_send(slot(xf, core, z_), sib, 28 + n)

    def q_group(x_):
        for z_ in range(4):
            r_wait(slot(x_, other, z_))
        raw = r_buf[pl.ds(x_ * 8, 8)].reshape(512, 512)
        moved = mm(perm[...], raw)
        r_k[...] = moved.astype(BF16)
        r_j[x_] = moved.T.astype(BF16)

        def q_step(ib, carry):
            block = mm(r_k[...], g[:, pl.ds(pl.multiple_of(ib * 256, 256), 256)]).astype(BF16)
            for d in range(32):
                for ii in range(2):
                    q[2 * ib + ii, x_, :, d * 128:(d + 1) * 128] = block[
                        d * 16:(d + 1) * 16, ii * 128:(ii + 1) * 128
                    ]
            return carry

        lax.fori_loop(0, 8, q_step, 0)

    q_group(xx)
    x_copy(xf, 0, xs).wait_recv()
    c_wait(xs, 2)
    s1[xs] = (core_sum(xs) + x_in[0].astype(F32)).astype(BF16)
    x_copy(xs, 2, xs).start()
    q_group(xm)
    q_group(xs)
    c_wait(xx, 3)
    x_copy(xm, 1, xm).wait_recv()
    x_copy(xs, 2, xs).wait_recv()
    s2[...] = (
        core_sum(xx) + x_in[1].astype(F32) + x_in[2].astype(F32)
    ).astype(BF16).reshape(4, 64, 512)

    def z_copy(z_, n, target_z):
        return remote(
            s2.at[z_], z_in.at[n], d_ss.at[7 + n], d_rs.at[7 + n], dev(target_z, xx, core)
        )

    z_copy(zf, 0, zs).start()
    z_copy(zm, 1, zm).start()
    q_group(xf)
    z_copy(zf, 0, zs).wait_recv()
    z_copy(zf, 0, zs).wait_send()
    s2[zs] = (s2[zs].astype(F32) + z_in[0].astype(F32)).astype(BF16)
    z_copy(zs, 2, zs).start()

    def lg_step(b, carry):
        rows = q[pl.ds(pl.multiple_of(b * 4, 4), 4)].reshape(256, 4096)
        lg_f[pl.ds(pl.multiple_of(b * 256, 256), 256), 0:32] = mm_nt(rows, w[...])
        return carry

    lax.fori_loop(0, 4, lg_step, 0)
    for s in range(32):
        base = (s // 8) * 16 + s % 8
        pieces = [
            lg_f[pl.ds(base + 8 * k, 16, stride=64), :][:, 0:32] for k in range(2)
        ]
        pieces.append(jnp.zeros((16, 64), F32))
        lg_out[s] = jnp.concatenate(pieces, axis=1).astype(BF16)

    def e_copy(k):
        s = lax.rem(mine + k, 32)
        return remote(lg_out.at[s], lg_in.at[me], e_ss.at[k], e_rs.at[me], slot_dev(s))

    def e_send(k, carry):
        e_copy(k).start()
        return carry

    lax.fori_loop(1, 32, e_send, 0)
    lg_in[me] = lg_out[mine]

    def rg_step(dp, carry):
        cols = pl.ds(pl.multiple_of(dp * 256, 256), 256)
        rg_l[:, cols] = mm(l_t[...], q[:, :, :, cols].reshape(1024, 256))
        return carry

    lax.fori_loop(0, 16, rg_step, 0)
    for d in range(32):
        rg_f[pl.ds(d, 32, stride=32), :] = rg_l[:, d * 128:(d + 1) * 128]
    rg_b[...] = rg_f[...].astype(BF16).reshape(2, 512, 128)
    a0 = remote(rg_b.at[other], ra, a_ss.at[0], a_rs.at[0], sib)
    a0.start()

    def u_step(ib, carry):
        cols = pl.ds(pl.multiple_of(ib * 256, 256), 256)
        acc = mm(r_j[0], t[0, :, :, cols].reshape(512, 256))
        for x in range(1, 4):
            acc = acc + mm(r_j[x], t[x, :, :, cols].reshape(512, 256))
        for ii in range(2):
            pair_o[2 * ib + ii] = (
                (acc[:, ii * 128:(ii + 1) * 128] + biases[...]) * rec[2 * ib + ii]
            ).astype(BF16)
        return carry

    lax.fori_loop(0, 4, u_step, 0)

    a0.wait_recv()
    rb[...] = (rg_b[core].astype(F32) + ra[...].astype(F32)).astype(BF16).reshape(4, 128, 128)

    def a_x(k):
        x_ = lax.rem(xx + k, 4)
        return remote(rb.at[x_], rc.at[xx], a_ss.at[k], a_rs.at[1 + xx], dev(zz, x_, core))

    for k in range(1, 4):
        a_x(k).start()
    rc[xx] = rb[xx]

    lax.fori_loop(4, 8, u_step, 0)

    for k in range(1, 4):
        x_ = lax.rem(xx + k, 4)
        remote(rb.at[x_], rc.at[x_], a_ss.at[k], a_rs.at[1 + x_], sib).wait_recv()
    rc_send[zz] = (
        (rc[0].astype(F32) + rc[1].astype(F32)) + (rc[2].astype(F32) + rc[3].astype(F32))
    ).astype(BF16)

    def a_z(k):
        z_ = lax.rem(zz + k, 4)
        return remote(
            rc_send.at[zz], rc_send.at[zz], a_ss.at[3 + k], a_rs.at[5 + zz], dev(z_, xx, core)
        )

    for k in range(1, 4):
        a_z(k).start()

    def e_wait(k, carry):
        p = lax.rem(me + k, 32)
        remote(lg_out.at[0], lg_in.at[p], e_ss.at[k], e_rs.at[p], sib).wait_recv()
        return carry

    lax.fori_loop(1, 32, e_wait, 0)
    z_copy(zm, 1, zm).wait_recv()
    z_copy(zs, 2, zs).wait_recv()
    right = s2[zz].astype(F32) + z_in[1].astype(F32) + z_in[2].astype(F32)
    right_t = right.T
    left = lg_in[...].reshape(512, 128).astype(F32)
    for k in range(2):
        both[k * 512:(k + 1) * 512, :] = jnp.concatenate(
            [left[:, k * 32:(k + 1) * 32], right_t[:, k * 32:(k + 1) * 32]], axis=1
        ) * mcol[k * 512:(k + 1) * 512, :]

    def grad_step(b, carry):
        sc_acc, sh_acc, of_acc, pj_acc = carry
        rows = pl.ds(pl.multiple_of(b * 128, 128), 128)
        pgb = both[rows, :].astype(BF16)
        ng = mm_nt(pgb, proj[...])
        standard = std[rows, :]
        pj_acc = pj_acc + mm_tn(pgb, normed[rows, :])
        of_acc = of_acc + jnp.sum(pgb.astype(F32), axis=0, keepdims=True)
        sc_acc = sc_acc + jnp.sum(ng * standard, axis=0, keepdims=True)
        sh_acc = sh_acc + jnp.sum(ng, axis=0, keepdims=True)
        h = ng * scales[...]
        m1 = jnp.mean(h, axis=-1, keepdims=True)
        m2 = jnp.mean(h * standard, axis=-1, keepdims=True)
        al_o[rows, :] = ((h - m1 - standard * m2) * inv[rows, :]).astype(BF16)
        return (sc_acc, sh_acc, of_acc, pj_acc)

    sc_acc, sh_acc, of_acc, pj_acc = lax.fori_loop(
        0, 8, grad_step,
        (jnp.zeros((1, 256), F32), jnp.zeros((1, 256), F32), jnp.zeros((1, 64), F32),
         jnp.zeros((64, 256), F32)),
    )
    pb[0] = pj_acc[0:40]
    pb[1, 0:24] = pj_acc[40:64]
    pb[1, 24:40] = jnp.concatenate(
        [
            sc_acc, sh_acc,
            jnp.concatenate([of_acc, jnp.zeros((1, 64), F32), bsum[...]], axis=1),
            jnp.zeros((13, 256), F32),
        ],
        axis=0,
    )

    b0 = remote(pb.at[other], pb_core, b_ss.at[0], b_rs.at[0], sib)
    b0.start()

    for k in range(1, 4):
        z_ = lax.rem(zz + k, 4)
        remote(
            rc_send.at[z_], rc_send.at[z_], a_ss.at[3 + k], a_rs.at[5 + z_], sib
        ).wait_recv()
    a_z(1).wait_send()
    rh[xx] = (
        (rc_send[0].astype(F32) + rc_send[1].astype(F32))
        + (rc_send[2].astype(F32) + rc_send[3].astype(F32))
    ).astype(BF16)

    def a_g(k):
        x_ = lax.rem(xx + k, 4)
        return remote(
            rh.at[xx], rh.at[xx], a_ss.at[6 + k], a_rs.at[9 + xx], dev(zz, x_, core)
        )

    for k in range(1, 4):
        a_g(k).start()

    b0.wait_recv()
    pb_x[xx] = pb[core] + pb_core[...]

    def b_x(k):
        x_ = lax.rem(xx + k, 4)
        return remote(pb_x.at[xx], pb_x.at[xx], b_ss.at[k], b_rs.at[1 + xx], dev(zz, x_, core))

    for k in range(1, 4):
        b_x(k).start()

    for k in range(1, 4):
        x_ = lax.rem(xx + k, 4)
        remote(rh.at[x_], rh.at[x_], a_ss.at[6 + k], a_rs.at[9 + x_], sib).wait_recv()
    a_last = remote(rh, rk, a_ss.at[10], a_rs.at[13], sib)
    a_last.start()

    for k in range(1, 4):
        x_ = lax.rem(xx + k, 4)
        remote(pb_x.at[x_], pb_x.at[x_], b_ss.at[k], b_rs.at[1 + x_], sib).wait_recv()
    pb_z[zz] = (pb_x[0] + pb_x[1]) + (pb_x[2] + pb_x[3])

    def b_z(k):
        z_ = lax.rem(zz + k, 4)
        return remote(
            pb_z.at[zz], pb_z.at[zz], b_ss.at[3 + k], b_rs.at[5 + zz], dev(z_, xx, core)
        )

    for k in range(1, 4):
        b_z(k).start()

    a_last.wait_recv()
    rg_o[pl.ds(pl.multiple_of(core * 512, 512), 512), :] = rh[...].reshape(512, 128).astype(F32)
    rg_o[pl.ds(pl.multiple_of(other * 512, 512), 512), :] = rk[...].reshape(512, 128).astype(F32)

    for k in range(1, 4):
        z_ = lax.rem(zz + k, 4)
        remote(pb_z.at[z_], pb_z.at[z_], b_ss.at[3 + k], b_rs.at[5 + z_], sib).wait_recv()
    pb_half[core] = (pb_z[0] + pb_z[1]) + (pb_z[2] + pb_z[3])
    b_last = remote(pb_half.at[core], pb_half.at[core], b_ss.at[7], b_rs.at[9], sib)
    b_last.start()

    for k in range(31):
        remote(r_buf.at[0], r_buf.at[0], r_ss.at[k], r_rs.at[0], sib).wait_send()

    def drain(k, carry):
        remote(l_out.at[0], l_in.at[0], l_ss.at[k], l_rs.at[0], sib).wait_send()
        remote(lg_out.at[0], lg_in.at[0], e_ss.at[k], e_rs.at[0], sib).wait_send()
        return carry

    lax.fori_loop(1, 32, drain, 0)
    for n, x_ in enumerate((xf, xm, xs, xx)):
        remote(d_buf.at[x_, other], c_in.at[x_], d_ss.at[n], d_rs.at[x_], sib).wait_send()
    x_copy(xf, 0, xs).wait_send()
    x_copy(xm, 1, xm).wait_send()
    x_copy(xs, 2, xs).wait_send()
    z_copy(zm, 1, zm).wait_send()
    z_copy(zs, 2, zs).wait_send()
    a0.wait_send()
    for k in range(1, 4):
        a_x(k).wait_send()
        a_g(k).wait_send()
        b_x(k).wait_send()
        b_z(k).wait_send()
    a_z(2).wait_send()
    a_z(3).wait_send()
    a_last.wait_send()
    b0.wait_send()

    remote(
        pb_half.at[other], pb_half.at[other], b_ss.at[7], b_rs.at[9], sib
    ).wait_recv()
    b_last.wait_send()
    pj = jnp.concatenate([pb_half[0], pb_half[1, 0:24]], axis=0)
    pg_o[...] = pj.T
    sg_o[...] = pb_half[1, 24:25, :]
    hg_o[...] = pb_half[1, 25:26, :]
    og_o[...] = pb_half[1, 26:27, 0:64]
    bg_o[...] = pb_half[1, 26:27, 128:256]


def per_device(
    alignment, alignment_mask, cotangent, scales, shifts, projection, offsets, readout, biases
):
    vmem = pl.BlockSpec(memory_space=pltpu.VMEM)
    shape = jax.ShapeDtypeStruct
    scratch = [
        pltpu.VMEM((1024, 1), F32),
        pltpu.VMEM((1024, 256), F32),
        pltpu.VMEM((1024, 1), F32),
        pltpu.VMEM((1024, 256), BF16),
        pltpu.VMEM((1024, 64), F32),
        pltpu.VMEM((32, 16, 128), BF16),
        pltpu.VMEM((32, 16, 128), BF16),
        pltpu.VMEM((512, 128), F32),
        pltpu.VMEM((1024, 32), BF16),
        pltpu.VMEM((32, 1024), BF16),
        pltpu.VMEM((32, 4096), BF16),
        pltpu.VMEM((1024, 128), F32),
        pltpu.VMEM((16, 512, 128), F32),
        pltpu.VMEM((512, 2048), BF16),
        pltpu.VMEM((512, 512), BF16),
        pltpu.VMEM((512, 512), BF16),
        pltpu.VMEM((32, 64, 512), BF16),
        pltpu.VMEM((512, 512), BF16),
        pltpu.VMEM((4, 512, 512), BF16),
        pltpu.VMEM((4, 32, 16, 2048), BF16),
        pltpu.VMEM((16, 4, 16, 4096), BF16),
        pltpu.VMEM((4, 2, 256, 512), BF16),
        pltpu.VMEM((4, 256, 512), BF16),
        pltpu.VMEM((4, 256, 512), BF16),
        pltpu.VMEM((3, 256, 512), BF16),
        pltpu.VMEM((4, 64, 512), BF16),
        pltpu.VMEM((3, 64, 512), BF16),
        pltpu.VMEM((1024, 128), F32),
        pltpu.VMEM((32, 16, 128), BF16),
        pltpu.VMEM((32, 16, 128), BF16),
        pltpu.VMEM((32, 4096), F32),
        pltpu.VMEM((1024, 128), F32),
        pltpu.VMEM((2, 512, 128), BF16),
        pltpu.VMEM((512, 128), BF16),
        pltpu.VMEM((4, 128, 128), BF16),
        pltpu.VMEM((4, 128, 128), BF16),
        pltpu.VMEM((4, 128, 128), BF16),
        pltpu.VMEM((4, 128, 128), BF16),
        pltpu.VMEM((4, 128, 128), BF16),
        pltpu.VMEM((2, 40, 256), F32),
        pltpu.VMEM((40, 256), F32),
        pltpu.VMEM((4, 40, 256), F32),
        pltpu.VMEM((8, 128), F32),
        pltpu.VMEM((4, 40, 256), F32),
        pltpu.VMEM((2, 40, 256), F32),
        pltpu.VMEM((8, 128), F32),
        pltpu.VMEM((1, 128), F32),
    ] + [pltpu.SemaphoreType.DMA((n,)) for n in (32, 32, 32, 32, 32, 32, 10, 10, 14, 14, 10, 10)]
    outs = pl.pallas_call(
        kernel,
        out_shape=(
            shape((16, 512, 128), BF16),
            shape((1024, 256), BF16),
            shape((256, 64), F32),
            shape((1, 64), F32),
            shape((1024, 128), F32),
            shape((1, 128), F32),
            shape((1, 256), F32),
            shape((1, 256), F32),
        ),
        in_specs=[vmem] * 9,
        out_specs=[vmem] * 8,
        scratch_shapes=scratch,
        compiler_params=pltpu.CompilerParams(
            collective_id=0, has_side_effects=True, vmem_limit_bytes=62 * 1024 * 1024
        ),
        cost_estimate=pl.CostEstimate(
            flops=16_000_000_000, bytes_accessed=6_000_000, transcendentals=0
        ),
        name="outer_product_mean",
    )(
        alignment.reshape(1024, 256),
        alignment_mask,
        cotangent,
        scales.reshape(1, 256),
        shifts.reshape(1, 256),
        projection,
        offsets.reshape(1, 64),
        readout,
        biases.reshape(1, 128),
    )
    return (
        outs[0],
        outs[1].reshape(2, 512, 256),
        outs[2],
        outs[3].reshape(64),
        outs[4],
        outs[5].reshape(128),
        outs[6].reshape(256),
        outs[7].reshape(256),
    )


def solution(mesh):
    return jax.shard_map(
        per_device,
        mesh=mesh,
        in_specs=(
            P(("crop", "dap"), None, None),
            P("crop", None),
            P(("crop", "dap"), None, None),
            P(),
            P(),
            P(),
            P(),
            P(),
            P(),
        ),
        out_specs=(
            P(("crop", "dap"), None, None),
            P(("crop", "dap"), None, None),
            P("crop", None),
            P("crop"),
            P("crop", None),
            P("crop"),
            P("crop"),
            P("crop"),
        ),
        check_vma=False,
    )
```

time: 787 us -> 101 us (0.13)
  waiting for transfers between devices: 431 us -> 0 us
  blocking collectives: 138 us -> 0 us
  Pallas kernels: 0 us -> 90.2 us
  matrix products: 77.4 us -> 0 us
  local copies, waits for them, and re-layouts: 76.8 us -> 10.1 us
  starting transfers between devices: 21.2 us -> 0 us
  between operations: 14.1 us -> 0.65 us
  other arithmetic: 13.4 us -> 0 us
  loops' own time: 7.96 us -> 0 us
    psum x1 -> x0, waiting for transfers between devices: 282 us -> none  [per_device(): lax.psum(readout_part.astype(jnp.bfloat16), 'dap').astype(jnp.float32)]
    psum x1 -> x0, blocking collectives: 138 us -> none  [per_device(): lax.psum(projection_part.astype(jnp.bfloat16), 'dap').astype(jnp.float32)]
    pallas_call x0 -> x1, Pallas kernels: none -> 90.2 us  [per_device(): pl.pallas_call(kernel, out_shape=(shape((16, 512, 128), BF16), shape((102...]
    reduce_scatter x1 -> x0, waiting for transfers between devices: 85 us -> none  [per_device(): lax.psum_scatter(partial_all.reshape(residues, sequences * channels).asty...]
    dot_general x28 -> x0, matrix products: 77.4 us -> none  [the longest x4 18.9 us: step_fn(): jnp.einsum('ijcd,jsd->sic', products_grad, right_piece, preferred_element...]
    all_gather x1 -> x0, waiting for transfers between devices: 46.3 us -> none  [per_device(): lax.all_gather(right_rows, 'dap', axis=0, tiled=True)]
    convert_element_type x9 -> x0, local copies, waits for them, and re-layouts: 36.6 us -> none  [the longest x4 25.7 us: step_fn(): products_grad.astype(jnp.bfloat16)]
    all_to_all x2 -> x0, starting transfers between devices: 21.1 us -> none  [the longest x1 12.6 us: per_device(): lax.all_to_all(alignment, 'dap', split_axis=1, concat_axis=0, tiled=True)]
  transfers between devices with their start and end apart: 5 -> 0, of which waited for: 4 -> 0; matrix products, arithmetic and copies ran while one was open for 2% -> 0% of each run, Pallas kernels for 0% -> 0%
where the time goes in v1:
time: 101 us
  Pallas kernels  90.2 us (89%)
  local copies, waits for them, and re-layouts  10.1 us (10%)
    pallas_call x1, Pallas kernels, per_device(): pl.pallas_call(kernel, out_shape=(shape((16, 512, 128), BF16), shape((102...  90.2 us
    unnamed x21, local copies, waits for them, and re-layouts  10.1 us

profile of v1, /device:TPU:1, one launch (start us, length us, event | category | flops | bytes accessed | tf_op | source)
XLA Modules:
  0.0 100.9 jit_solution(5521793090077137574)
XLA Ops:
  0.6 1.5 %copy.17.proj = bf16[256,64]{1,0:T(8,128)(2,1)} copy(bf16[256,64]{0,1:T(8,128)(2,1)} %param.14) | data formatting | bytes 65536 | tf_op args[5]
  2.1 90.2 %outer_product_mean.1 = (bf16[16,512,128]{2,1,0:T(8,128)(2,1)}, bf16[1024,256]{1,0:T(8,128)(2,1)}, f32[256,64]{1,0:T(8,128)}, f32[1,64]{1,0:T(1,128)}, f32[1024,...) custom-call(bf16[1024,256]{1,0:T(8,128)(2,1)} %bitcast.13, s32[64,512]{1,0:T(8,128)} %mask.1, ...), custom_call_target="tpu_custom_call" | custom-call | flops 16000000000 | bytes 6000000 | tf_op jit(solution)/shard_map/outer_product_mean/pallas_call | solution.py:577
  92.3 1.6 %copy.18 = f32[256,64]{0,1:T(8,128)} copy(f32[256,64]{1,0:T(8,128)} %get-tuple-element.26) | data formatting | bytes 131072
  93.9 0.0 copy-start.1
  93.9 0.0 copy-start.5
  93.9 0.0 copy-start
  93.9 3.2 %copy.26 = bf16[16,512,128]{2,1,0:T(8,128)(2,1)} copy(bf16[16,512,128]{2,1,0:T(8,128)(2,1)} %get-tuple-element.40) | data formatting | bytes 4194304
  97.1 0.0 copy-done.1
  97.1 0.0 copy-start.4
  97.1 0.0 copy-start.3
  97.1 0.0 copy-start.2
  97.1 0.8 copy.27
  97.9 0.0 copy-done.5
  97.9 0.5 copy.28
  98.5 0.0 copy-done
  98.5 0.8 copy.29
  99.2 0.0 copy-done.4
  99.3 0.5 copy.30
  99.8 0.0 copy-done.3
  99.8 0.6 copy.31
  100.3 0.0 copy-done.2
  100.3 0.6 copy.32
Async XLA Ops:
  93.9 3.2 %copy-start.1 = (bf16[1024,256]{1,0:T(8,128)(2,1)S(1)}, bf16[1024,256]{1,0:T(8,128)(2,1)}, u32[]{:S(2)}) copy-start(bf16[1024,256]{1,0:T(8,128)(2,1)} %get-tuple-element.17) | copy-start | bytes 1572868
  93.9 4.0 %copy-start.5 = (f32[1,64]{1,0:T(1,128)S(1)}, f32[1,64]{1,0:T(1,128)}, u32[]{:S(2)}) copy-start(f32[1,64]{1,0:T(1,128)} %get-tuple-element.19) | copy-start | bytes 772
  93.9 4.5 %copy-start = (f32[1024,128]{1,0:T(8,128)S(1)}, f32[1024,128]{1,0:T(8,128)}, u32[]{:S(2)}) copy-start(f32[1024,128]{1,0:T(8,128)} %get-tuple-element.44) | copy-start | bytes 1572868
  97.1 2.1 %copy-start.4 = (f32[1,128]{1,0:T(1,128)S(1)}, f32[1,128]{1,0:T(1,128)}, u32[]{:S(2)}) copy-start(f32[1,128]{1,0:T(1,128)} %get-tuple-element.21) | copy-start | bytes 1540
  97.1 2.6 %copy-start.3 = (f32[1,256]{1,0:T(1,128)S(1)}, f32[1,256]{1,0:T(1,128)}, u32[]{:S(2)}) copy-start(f32[1,256]{1,0:T(1,128)} %get-tuple-element.22) | copy-start | bytes 3076
  97.1 3.2 %copy-start.2 = (f32[1,256]{1,0:T(1,128)S(1)}, f32[1,256]{1,0:T(1,128)}, u32[]{:S(2)}) copy-start(f32[1,256]{1,0:T(1,128)} %get-tuple-element.23) | copy-start | bytes 3076

commit v2 on v1

v2 whole, which is shorter than its diff:
```python
import jax
import jax.numpy as jnp
from jax import lax
from jax.experimental import pallas as pl
from jax.experimental.pallas import tpu as pltpu
from jax.sharding import PartitionSpec as P

F32 = jnp.float32
BF16 = jnp.bfloat16
MESH = pl.DeviceIdType.MESH


def mm(a, b):
    return lax.dot_general(a, b, (((1,), (0,)), ((), ())), preferred_element_type=F32)


def mm_nt(a, b):
    return lax.dot_general(a, b, (((1,), (1,)), ((), ())), preferred_element_type=F32)


def mm_tn(a, b):
    return lax.dot_general(a, b, (((0,), (0,)), ((), ())), preferred_element_type=F32)


def iota(shape, dim):
    return lax.broadcasted_iota(jnp.int32, shape, dim)


def kernel(
    al, mask, cot, scales, shifts, proj, offs, readout, biases,
    pair_o, al_o, pg_o, og_o, rg_o, bg_o, sg_o, hg_o,
    cot_v, pair_v, al_v, mcol, std, inv, normed, both, l_out, l_in, l_f, l_all, l_t, w, ro_f,
    rec, g, perm, perm_t, r_buf, r_k, r_j, t, q,
    d_buf, c_in, s1, x_in, s2, z_in,
    lg_f, lg_out, lg_in, rg_l, rg_f, rg_b, ra, rb, rc, re, rh, rk,
    ng_s, pb, pb_core, pb_x, pb_z, pb_half, bsum,
    l_ss, l_rs, e_ss, e_rs, r_ss, r_rs, d_ss, d_rs, a_ss, a_rs, b_ss, b_rs, io,
):
    me = lax.axis_index("dap")
    core = lax.rem(me, 2)
    xx = lax.rem(lax.div(me, 2), 4)
    zz = lax.div(me, 8)
    sign = 1 - 2 * core
    xs, xm, xf = (lax.rem(xx + 4 + sign, 4), lax.rem(xx + 4 - sign, 4), lax.rem(xx + 2, 4))
    zs, zm, zf = (lax.rem(zz + 4 + sign, 4), lax.rem(zz + 4 - sign, 4), lax.rem(zz + 2, 4))
    other = 1 - core

    def dev(z, x, c):
        return (z * 4 + x) * 2 + c

    def slot(x, c, z):
        return (x * 2 + c) * 4 + z

    def slot_dev(s):
        return dev(lax.rem(s, 4), lax.div(s, 8), lax.rem(lax.div(s, 4), 2))

    sib = dev(zz, xx, other)
    mine = slot(xx, core, zz)

    def remote(src, dst, ss, rs, target):
        return pltpu.make_async_remote_copy(
            src_ref=src, dst_ref=dst, send_sem=ss, recv_sem=rs,
            device_id={"dap": target}, device_id_type=MESH,
        )

    barrier = pltpu.get_barrier_semaphore()

    def greet(k, carry):
        pl.semaphore_signal(
            barrier, inc=1, device_id={"dap": lax.rem(me + k, 32)}, device_id_type=MESH
        )
        return carry

    lax.fori_loop(1, 32, greet, 0)
    cot_copy = pltpu.make_async_copy(cot, cot_v, io.at[0])
    cot_copy.start()

    mask_f = mask[...].astype(F32)
    mask_t = mask_f.T
    for k in range(2):
        mcol[k * 512:(k + 1) * 512, :] = jnp.sum(
            jnp.where(iota((512, 64), 1) == 2 * me + k, mask_t, 0.0), axis=1, keepdims=True
        )
    for k in range(2):
        rows = slice(k * 512, (k + 1) * 512)
        wide = al[rows, :].astype(F32)
        center = jnp.mean(wide, axis=-1, keepdims=True)
        apart = wide - center
        spread = jnp.mean(apart * apart, axis=-1, keepdims=True)
        inverse = lax.rsqrt(spread + 1e-05)
        standard = apart * inverse
        std[rows, :] = standard
        inv[rows, :] = inverse
        normed[rows, :] = (standard * scales[...] + shifts[...]).astype(BF16)
    both[...] = (mm_nt(normed[...], proj[...]) + offs[...]) * mcol[...]
    cat = jnp.concatenate([both[0:512, :], both[512:1024, :]], axis=1)
    l_out[...] = cat.astype(BF16).reshape(32, 16, 128)
    cat_t = cat.T
    r_buf[mine] = jnp.concatenate([cat_t[32:64], cat_t[96:128]], axis=0).astype(BF16)

    pl.semaphore_wait(barrier, 31)

    def l_send(k, carry):
        s = lax.rem(mine + k, 32)
        p = slot_dev(s)
        remote(l_out.at[p], l_in.at[mine], l_ss.at[k], l_rs.at[mine], p).start()
        return carry

    lax.fori_loop(1, 32, l_send, 0)

    def r_send(s, target, k):
        remote(r_buf.at[s], r_buf.at[s], r_ss.at[k], r_rs.at[s], target).start()

    def r_wait(s):
        remote(r_buf.at[s], r_buf.at[s], r_ss.at[0], r_rs.at[s], sib).wait_recv()

    r_send(mine, dev(zs, xx, core), 0)
    r_send(mine, dev(zm, xx, core), 1)
    r_send(mine, dev(zz, xs, core), 2)
    r_send(mine, dev(zz, xm, core), 3)
    r_send(mine, sib, 4)
    l_in[mine] = l_out[me]

    mask_b = mask_f.astype(BF16)
    own_cols = (iota((512, 16), 0) == 16 * me + iota((512, 16), 1)).astype(F32).astype(BF16)
    mask_own = mm(mask_b, own_cols).astype(BF16)
    recip = 1.0 / (0.001 + mm(mask_t.astype(BF16), mask_own))
    total = jnp.zeros((1, 128), F32)
    cot_copy.wait()
    for i in range(16):
        rec_i = jnp.broadcast_to(recip[:, i:i + 1], (512, 128))
        rec[i] = rec_i
        sg = (cot_v[i].astype(F32) * rec_i).astype(BF16)
        g[:, i * 128:(i + 1) * 128] = sg
        total = total + jnp.sum(sg.astype(F32), axis=0, keepdims=True)
    bsum[...] = total

    ro_f[...] = readout[...].astype(F32)
    for d in range(32):
        w[:, d * 128:(d + 1) * 128] = ro_f[pl.ds(d, 32, stride=32), :].astype(BF16)

    def packed(a):
        return lax.rem(a, 8) * 64 + lax.rem(lax.div(a, 8), 2) * 32 + lax.div(a, 16)

    perm[...] = (iota((512, 512), 1) == packed(iota((512, 512), 0))).astype(F32).astype(BF16)
    perm_t[...] = (iota((512, 512), 0) == packed(iota((512, 512), 1))).astype(F32).astype(BF16)

    def l_wait(k, carry):
        s = lax.rem(mine + k, 32)
        remote(l_out.at[0], l_in.at[s], l_ss.at[k], l_rs.at[s], sib).wait_recv()
        return carry

    lax.fori_loop(1, 32, l_wait, 0)
    l_f[...] = l_in[...].reshape(512, 128).astype(F32)
    for i in range(16):
        v = l_f[pl.ds(i, 32, stride=16), :]
        for x in range(4):
            part = v[x * 8:x * 8 + 8, :]
            l_all[x * 256 + i * 16:x * 256 + (i + 1) * 16, :] = jnp.concatenate(
                [part[:, 0:32], part[:, 64:96]], axis=0
            ).astype(BF16)
    l_t[...] = l_all[...].astype(F32).T.astype(BF16)

    def t_group(x_):
        r = mm(l_all[pl.ds(pl.multiple_of(x_ * 256, 256), 256), :], w[...]).astype(BF16)
        for d in range(32):
            t[x_, :, d] = r[:, d * 128:(d + 1) * 128].reshape(16, 16, 128)

    def d_group(x_, n):
        rows = jnp.concatenate([t[x_, i].reshape(512, 128) for i in range(16)], axis=1)
        raw = mm_nt(rows, g[...]).astype(BF16)
        d_buf[x_] = mm(perm_t[...], raw).astype(BF16).reshape(2, 256, 512)
        remote(d_buf.at[x_, other], c_in.at[x_], d_ss.at[n], d_rs.at[x_], sib).start()

    def c_wait(x_, n):
        remote(d_buf.at[x_, other], c_in.at[x_], d_ss.at[n], d_rs.at[x_], sib).wait_recv()

    def core_sum(x_):
        return d_buf[x_, core].astype(F32) + c_in[x_].astype(F32)

    def x_copy(x_, n, target_x):
        return remote(
            s1.at[x_], x_in.at[n], d_ss.at[4 + n], d_rs.at[4 + n], dev(zz, target_x, core)
        )

    t_group(xf)
    r_wait(slot(xx, core, zm))
    r_send(slot(xx, core, zm), dev(zs, xx, core), 5)
    for n, z_ in enumerate((zm, zs)):
        if n == 1:
            r_wait(slot(xx, core, z_))
        r_send(slot(xx, core, z_), dev(zz, xs, core), 6 + 3 * n)
        r_send(slot(xx, core, z_), dev(zz, xm, core), 7 + 3 * n)
        r_send(slot(xx, core, z_), sib, 8 + 3 * n)
    d_group(xf, 0)
    r_wait(slot(xm, core, zz))
    r_send(slot(xm, core, zz), dev(zz, xs, core), 15)
    r_send(slot(xm, core, zz), sib, 16)
    r_wait(slot(xs, core, zz))
    r_send(slot(xs, core, zz), sib, 17)
    t_group(xm)
    r_wait(slot(xx, core, zf))
    r_send(slot(xx, core, zf), dev(zz, xs, core), 12)
    r_send(slot(xx, core, zf), dev(zz, xm, core), 13)
    r_send(slot(xx, core, zf), sib, 14)
    d_group(xm, 1)
    c_wait(xf, 0)
    s1[xf] = core_sum(xf).astype(BF16)
    x_copy(xf, 0, xs).start()
    for n, z_ in enumerate((zm, zs)):
        r_wait(slot(xm, core, z_))
        r_send(slot(xm, core, z_), dev(zz, xs, core), 18 + 3 * n)
        r_send(slot(xm, core, z_), sib, 19 + 3 * n)
        r_wait(slot(xs, core, z_))
        r_send(slot(xs, core, z_), sib, 20 + 3 * n)
    t_group(xs)
    d_group(xs, 2)
    c_wait(xm, 1)
    s1[xm] = core_sum(xm).astype(BF16)
    x_copy(xm, 1, xm).start()
    r_wait(slot(xm, core, zf))
    r_send(slot(xm, core, zf), dev(zz, xs, core), 24)
    r_send(slot(xm, core, zf), sib, 25)
    r_wait(slot(xs, core, zf))
    r_send(slot(xs, core, zf), sib, 26)
    r_wait(slot(xf, core, zz))
    r_send(slot(xf, core, zz), sib, 27)
    t_group(xx)
    d_group(xx, 3)
    for n, z_ in enumerate((zm, zs, zf)):
        r_wait(slot(xf, core, z_))
        r_send(slot(xf, core, z_), sib, 28 + n)

    def r_prep(x_):
        for z_ in range(4):
            r_wait(slot(x_, other, z_))
        raw = r_buf[pl.ds(x_ * 8, 8)].reshape(512, 512)
        moved = mm(perm[...], raw)
        r_k[...] = moved.astype(BF16)
        r_j[:, pl.ds(pl.multiple_of(x_ * 512, 512), 512)] = moved.T.astype(BF16)

    def e_copy(s, k):
        return remote(lg_out.at[s], lg_in.at[me], e_ss.at[k], e_rs.at[me], slot_dev(s))

    def q_group(x_, n):
        for h in range(2):
            block = mm(r_k[...], g[:, h * 1024:(h + 1) * 1024]).astype(BF16)
            for i in range(8):
                q[x_, h * 8 + i] = block[:, i * 128:(i + 1) * 128].reshape(32, 16, 128)
        rows = jnp.concatenate([q[x_, :, d].reshape(256, 128) for d in range(32)], axis=1)
        lg_f[:, 0:32] = mm_nt(rows, w[...])
        for c in range(8):
            pieces = [lg_f[pl.ds(c + 8 * k, 16, stride=16), :][:, 0:32] for k in range(2)]
            pieces.append(jnp.zeros((16, 64), F32))
            lg_out[x_ * 8 + c] = jnp.concatenate(pieces, axis=1).astype(BF16)
        if n == 0:
            for k in range(1, 8):
                e_copy(x_ * 8 + lax.rem(core * 4 + zz + k, 8), k).start()
            lg_in[me] = lg_out[mine]
        else:
            for k in range(8):
                e_copy(x_ * 8 + k, n * 8 + k).start()

    def z_copy(k):
        z_ = lax.rem(zz + k, 4)
        return remote(
            s2.at[z_], z_in.at[zz], d_ss.at[6 + k], d_rs.at[7 + zz], dev(z_, xx, core)
        )

    r_prep(xx)
    c_wait(xs, 2)
    x_copy(xf, 0, xs).wait_recv()
    s1[xs] = (core_sum(xs) + x_in[0].astype(F32)).astype(BF16)
    x_copy(xs, 2, xs).start()
    q_group(xx, 0)
    r_prep(xm)
    q_group(xm, 1)
    c_wait(xx, 3)
    x_copy(xm, 1, xm).wait_recv()
    x_copy(xs, 2, xs).wait_recv()
    s2[...] = (
        core_sum(xx) + x_in[1].astype(F32) + x_in[2].astype(F32)
    ).astype(BF16).reshape(4, 64, 512)
    for k in range(1, 4):
        z_copy(k).start()
    r_prep(xs)
    q_group(xs, 2)
    r_prep(xf)
    q_group(xf, 3)

    rows_q = jnp.concatenate(
        [q[:, :, d].reshape(1024, 128) for d in range(32)], axis=1
    )
    rg_l[...] = mm(l_t[...], rows_q)
    for d in range(32):
        rg_f[pl.ds(d, 32, stride=32), :] = rg_l[:, d * 128:(d + 1) * 128]
    rg_b[...] = rg_f[...].astype(BF16).reshape(2, 512, 128)
    a0 = remote(rg_b.at[other], ra, a_ss.at[0], a_rs.at[0], sib)
    a0.start()

    def pair_copy(ib):
        return pltpu.make_async_copy(
            pair_v.at[pl.ds(ib * 4, 4)], pair_o.at[pl.ds(ib * 4, 4)], io.at[ib + 1]
        )

    def u_step(ib):
        cols = jnp.concatenate(
            [t[:, ib * 4 + ii].reshape(2048, 128) for ii in range(4)], axis=1
        )
        acc = mm(r_j[...], cols)
        for ii in range(4):
            pair_v[4 * ib + ii] = (
                (acc[:, ii * 128:(ii + 1) * 128] + biases[...]) * rec[4 * ib + ii]
            ).astype(BF16)
        pair_copy(ib).start()

    u_step(0)
    u_step(1)

    a0.wait_recv()
    rb[...] = (rg_b[core].astype(F32) + ra[...].astype(F32)).astype(BF16).reshape(4, 128, 128)

    def a_x(k):
        x_ = lax.rem(xx + k, 4)
        return remote(rb.at[x_], rc.at[xx], a_ss.at[k], a_rs.at[1 + xx], dev(zz, x_, core))

    for k in range(1, 4):
        a_x(k).start()
    rc[xx] = rb[xx]

    for k in range(1, 32):
        p = lax.rem(me + k, 32)
        remote(lg_out.at[0], lg_in.at[p], e_ss.at[k], e_rs.at[p], sib).wait_recv()
    for k in range(1, 4):
        z_ = lax.rem(zz + k, 4)
        remote(s2.at[z_], z_in.at[z_], d_ss.at[6 + k], d_rs.at[7 + z_], sib).wait_recv()
    z_in[zz] = s2[zz]
    right = (z_in[0].astype(F32) + z_in[1].astype(F32)) + (
        z_in[2].astype(F32) + z_in[3].astype(F32)
    )
    right_t = right.T
    left = lg_in[...].reshape(512, 128).astype(F32)
    for k in range(2):
        both[k * 512:(k + 1) * 512, :] = jnp.concatenate(
            [left[:, k * 32:(k + 1) * 32], right_t[:, k * 32:(k + 1) * 32]], axis=1
        ) * mcol[k * 512:(k + 1) * 512, :]
    pgb = both[...].astype(BF16)
    pj_acc = mm_tn(pgb, normed[...])
    of_acc = jnp.sum(pgb.astype(F32), axis=0, keepdims=True)
    ng_s[...] = mm(pgb, proj[...])
    sc_acc = jnp.sum(ng_s[...] * std[...], axis=0, keepdims=True)
    sh_acc = jnp.sum(ng_s[...], axis=0, keepdims=True)
    pb[0] = pj_acc[0:48].astype(BF16)
    pb[1] = jnp.concatenate(
        [
            pj_acc[48:64], sc_acc, sh_acc,
            jnp.concatenate([of_acc, jnp.zeros((1, 64), F32), bsum[...]], axis=1),
            jnp.zeros((29, 256), F32),
        ],
        axis=0,
    ).astype(BF16)
    b0 = remote(pb.at[other], pb_core, b_ss.at[0], b_rs.at[0], sib)
    b0.start()

    for k in range(1, 4):
        x_ = lax.rem(xx + k, 4)
        remote(rb.at[x_], rc.at[x_], a_ss.at[k], a_rs.at[1 + x_], sib).wait_recv()

    def four(ref):
        return (ref[0].astype(F32) + ref[1].astype(F32)) + (
            ref[2].astype(F32) + ref[3].astype(F32)
        )

    re[zz] = four(rc).astype(BF16)

    def a_z(k):
        z_ = lax.rem(zz + k, 4)
        return remote(re.at[zz], re.at[zz], a_ss.at[3 + k], a_rs.at[5 + zz], dev(z_, xx, core))

    for k in range(1, 4):
        a_z(k).start()

    b0.wait_recv()
    pb_x[xx] = (pb[core].astype(F32) + pb_core[...].astype(F32)).astype(BF16)

    def b_x(k):
        x_ = lax.rem(xx + k, 4)
        return remote(pb_x.at[xx], pb_x.at[xx], b_ss.at[k], b_rs.at[1 + xx], dev(zz, x_, core))

    for k in range(1, 4):
        b_x(k).start()

    for b in range(4):
        rows = slice(b * 256, (b + 1) * 256)
        h = ng_s[rows, :] * scales[...]
        standard = std[rows, :]
        m1 = jnp.mean(h, axis=-1, keepdims=True)
        m2 = jnp.mean(h * standard, axis=-1, keepdims=True)
        al_v[rows, :] = ((h - m1 - standard * m2) * inv[rows, :]).astype(BF16)
    al_copy = pltpu.make_async_copy(al_v, al_o, io.at[5])
    al_copy.start()
    u_step(2)

    for k in range(1, 4):
        z_ = lax.rem(zz + k, 4)
        remote(re.at[z_], re.at[z_], a_ss.at[3 + k], a_rs.at[5 + z_], sib).wait_recv()
    rh[xx] = four(re).astype(BF16)

    def a_g(k):
        x_ = lax.rem(xx + k, 4)
        return remote(rh.at[xx], rh.at[xx], a_ss.at[6 + k], a_rs.at[9 + xx], dev(zz, x_, core))

    for k in range(1, 4):
        a_g(k).start()

    for k in range(1, 4):
        x_ = lax.rem(xx + k, 4)
        remote(pb_x.at[x_], pb_x.at[x_], b_ss.at[k], b_rs.at[1 + x_], sib).wait_recv()
    pb_z[zz] = four(pb_x).astype(BF16)

    def b_z(k):
        z_ = lax.rem(zz + k, 4)
        return remote(
            pb_z.at[zz], pb_z.at[zz], b_ss.at[3 + k], b_rs.at[5 + zz], dev(z_, xx, core)
        )

    for k in range(1, 4):
        b_z(k).start()
    u_step(3)

    for k in range(1, 4):
        x_ = lax.rem(xx + k, 4)
        remote(rh.at[x_], rh.at[x_], a_ss.at[6 + k], a_rs.at[9 + x_], sib).wait_recv()
    a_last = remote(rh, rk, a_ss.at[10], a_rs.at[13], sib)
    a_last.start()
    rg_o[pl.ds(pl.multiple_of(core * 512, 512), 512), :] = rh[...].reshape(512, 128).astype(F32)

    for k in range(1, 4):
        z_ = lax.rem(zz + k, 4)
        remote(pb_z.at[z_], pb_z.at[z_], b_ss.at[3 + k], b_rs.at[5 + z_], sib).wait_recv()
    pb_half[core] = four(pb_z).astype(BF16)
    b_last = remote(pb_half.at[core], pb_half.at[core], b_ss.at[7], b_rs.at[9], sib)
    b_last.start()

    def drain(k, carry):
        remote(l_out.at[0], l_in.at[0], l_ss.at[k], l_rs.at[0], sib).wait_send()
        remote(lg_out.at[0], lg_in.at[0], e_ss.at[k], e_rs.at[0], sib).wait_send()
        remote(r_buf.at[0], r_buf.at[0], r_ss.at[k - 1], r_rs.at[0], sib).wait_send()
        return carry

    lax.fori_loop(1, 32, drain, 0)
    for n, x_ in enumerate((xf, xm, xs, xx)):
        remote(d_buf.at[x_, other], c_in.at[x_], d_ss.at[n], d_rs.at[x_], sib).wait_send()
    x_copy(xf, 0, xs).wait_send()
    x_copy(xm, 1, xm).wait_send()
    x_copy(xs, 2, xs).wait_send()
    a0.wait_send()
    b0.wait_send()
    for k in range(1, 4):
        z_copy(k).wait_send()
        a_x(k).wait_send()
        a_z(k).wait_send()
        a_g(k).wait_send()
        b_x(k).wait_send()
        b_z(k).wait_send()
    for ib in range(4):
        pair_copy(ib).wait()
    al_copy.wait()
    a_last.wait()
    rg_o[pl.ds(pl.multiple_of(other * 512, 512), 512), :] = rk[...].reshape(512, 128).astype(F32)
    remote(
        pb_half.at[other], pb_half.at[other], b_ss.at[7], b_rs.at[9], sib
    ).wait_recv()
    b_last.wait_send()
    pg_o[...] = jnp.concatenate([pb_half[0], pb_half[1, 0:16]], axis=0).astype(F32)
    vec = pb_half[1, 16:32].astype(F32)
    sg_o[...] = vec[0:1, :]
    hg_o[...] = vec[1:2, :]
    og_o[...] = vec[2:3, 0:64]
    bg_o[...] = vec[2:3, 128:256]


def finish(*refs):
    srcs, dsts, sems = refs[0:8], refs[8:16], refs[16]
    copies = [
        pltpu.make_async_copy(srcs[0].at[pl.ds(4 * n, 4)], dsts[0].at[pl.ds(4 * n, 4)], sems.at[n])
        for n in range(4)
    ]
    copies += [
        pltpu.make_async_copy(srcs[n], dsts[n], sems.at[3 + n]) for n in range(1, 8)
    ]
    for copy in copies:
        copy.start()
    for copy in copies:
        copy.wait()


def per_device(
    alignment, alignment_mask, cotangent, scales, shifts, projection, offsets, readout, biases
):
    vmem = pl.BlockSpec(memory_space=pltpu.VMEM)
    shape = jax.ShapeDtypeStruct
    sizes = dict(
        cot_v=((16, 512, 128), BF16),
        pair_v=((16, 512, 128), BF16),
        al_v=((1024, 256), BF16),
        mcol=((1024, 1), F32),
        std=((1024, 256), F32),
        inv=((1024, 1), F32),
        normed=((1024, 256), BF16),
        both=((1024, 64), F32),
        l_out=((32, 16, 128), BF16),
        l_in=((32, 16, 128), BF16),
        l_f=((512, 128), F32),
        l_all=((1024, 32), BF16),
        l_t=((32, 1024), BF16),
        w=((32, 4096), BF16),
        ro_f=((1024, 128), F32),
        rec=((16, 512, 128), F32),
        g=((512, 2048), BF16),
        perm=((512, 512), BF16),
        perm_t=((512, 512), BF16),
        r_buf=((32, 64, 512), BF16),
        r_k=((512, 512), BF16),
        r_j=((512, 2048), BF16),
        t=((4, 16, 32, 16, 128), BF16),
        q=((4, 16, 32, 16, 128), BF16),
        d_buf=((4, 2, 256, 512), BF16),
        c_in=((4, 256, 512), BF16),
        s1=((4, 256, 512), BF16),
        x_in=((3, 256, 512), BF16),
        s2=((4, 64, 512), BF16),
        z_in=((4, 64, 512), BF16),
        lg_f=((256, 128), F32),
        lg_out=((32, 16, 128), BF16),
        lg_in=((32, 16, 128), BF16),
        rg_l=((32, 4096), F32),
        rg_f=((1024, 128), F32),
        rg_b=((2, 512, 128), BF16),
        ra=((512, 128), BF16),
        rb=((4, 128, 128), BF16),
        rc=((4, 128, 128), BF16),
        re=((4, 128, 128), BF16),
        rh=((4, 128, 128), BF16),
        rk=((4, 128, 128), BF16),
        ng_s=((1024, 256), F32),
        pb=((2, 48, 256), BF16),
        pb_core=((48, 256), BF16),
        pb_x=((4, 48, 256), BF16),
        pb_z=((4, 48, 256), BF16),
        pb_half=((2, 48, 256), BF16),
        bsum=((1, 128), F32),
    )
    scratch = [pltpu.VMEM(*size) for size in sizes.values()] + [
        pltpu.SemaphoreType.DMA((n,)) for n in (32, 32, 32, 32, 31, 32, 10, 11, 11, 14, 8, 10, 6)
    ]
    anywhere = pl.BlockSpec(memory_space=pl.ANY)
    outs = pl.pallas_call(
        kernel,
        out_shape=(
            shape((16, 512, 128), BF16),
            shape((1024, 256), BF16),
            shape((64, 256), F32),
            shape((1, 64), F32),
            shape((1024, 128), F32),
            shape((1, 128), F32),
            shape((1, 256), F32),
            shape((1, 256), F32),
        ),
        in_specs=[vmem] * 2 + [anywhere] + [vmem] * 6,
        out_specs=[anywhere] * 2 + [vmem] * 6,
        scratch_shapes=scratch,
        compiler_params=pltpu.CompilerParams(
            collective_id=0, has_side_effects=True, vmem_limit_bytes=62 * 1024 * 1024
        ),
        cost_estimate=pl.CostEstimate(
            flops=16_000_000_000, bytes_accessed=6_000_000, transcendentals=0
        ),
        name="outer_product_mean",
    )(
        alignment.reshape(1024, 256),
        alignment_mask,
        cotangent,
        scales.reshape(1, 256),
        shifts.reshape(1, 256),
        projection.T,
        offsets.reshape(1, 64),
        readout,
        biases.reshape(1, 128),
    )
    outs = pl.pallas_call(
        finish,
        out_shape=tuple(shape(out.shape, out.dtype) for out in outs),
        in_specs=[anywhere] * 8,
        out_specs=[anywhere] * 8,
        scratch_shapes=[pltpu.SemaphoreType.DMA((11,))],
        name="results",
    )(*outs)
    return (
        outs[0],
        outs[1].reshape(2, 512, 256),
        outs[2].T,
        outs[3].reshape(64),
        outs[4],
        outs[5].reshape(128),
        outs[6].reshape(256),
        outs[7].reshape(256),
    )


def solution(mesh):
    return jax.shard_map(
        per_device,
        mesh=mesh,
        in_specs=(
            P(("crop", "dap"), None, None),
            P("crop", None),
            P(("crop", "dap"), None, None),
            P(),
            P(),
            P(),
            P(),
            P(),
            P(),
        ),
        out_specs=(
            P(("crop", "dap"), None, None),
            P(("crop", "dap"), None, None),
            P("crop", None),
            P("crop"),
            P("crop", None),
            P("crop"),
            P("crop"),
            P("crop"),
        ),
        check_vma=False,
    )
```

time: 101 us -> 172 us (1.70)
  Pallas kernels: 90.2 us -> 171 us
  local copies, waits for them, and re-layouts: 10.1 us -> 0 us
    pallas_call x0 -> x1, Pallas kernels: none -> 98.6 us  [per_device(): pl.pallas_call(finish, out_shape=tuple((shape(out.shape, out.dtype) for o...]
    pallas_call x1, Pallas kernels: 90.2 us -> 72.7 us  [per_device(): pl.pallas_call(kernel, out_shape=(shape((16, 512, 128), BF16), shape((102...]
    unnamed x21 -> x0, local copies, waits for them, and re-layouts: 10.1 us -> none
where the time goes in v2:
time: 172 us
  Pallas kernels  171 us (99%)
    pallas_call x1, Pallas kernels, per_device(): pl.pallas_call(finish, out_shape=tuple((shape(out.shape, out.dtype) for o...  98.6 us
    pallas_call x1, Pallas kernels, per_device(): pl.pallas_call(kernel, out_shape=(shape((16, 512, 128), BF16), shape((102...  72.7 us

profile of v2, /device:TPU:1, one launch (start us, length us, event | category | flops | bytes accessed | tf_op | source)
XLA Modules:
  0.0 172.1 jit_solution(15268765557054911296)
XLA Ops:
  0.6 72.7 %outer_product_mean.1 = (bf16[16,512,128]{2,1,0:T(8,128)(2,1)}, bf16[1024,256]{1,0:T(8,128)(2,1)}, f32[64,256]{1,0:T(8,128)}, f32[1,64]{1,0:T(1,128)}, f32[1024,...) custom-call(bf16[1024,256]{1,0:T(8,128)(2,1)} %bitcast.12, s32[64,512]{1,0:T(8,128)} %mask.1, ...), custom_call_target="tpu_custom_call" | custom-call | flops 16000000000 | bytes 6000000 | tf_op jit(solution)/shard_map/outer_product_mean/pallas_call | solution.py:558
  73.3 98.6 %results.1 = (bf16[16,512,128]{2,1,0:T(8,128)(2,1)}, bf16[1024,256]{1,0:T(8,128)(2,1)}, f32[64,256]{1,0:T(8,128)}, f32[1,64]{1,0:T(1,128)}, f32[1024,128]{1,0:T(...) custom-call(bf16[16,512,128]{2,1,0:T(8,128)(2,1)} %get-tuple-element.24.refs_0_, ...), custom_call_target="tpu_custom_call" | custom-call | tf_op jit(solution)/shard_map/results/pallas_call | solution.py:591

commit v3 on v2

--- a/solution.py
+++ b/solution.py
@@ -481,18 +481,18 @@
 
 
 def finish(*refs):
-    srcs, dsts, sems = refs[0:8], refs[8:16], refs[16]
-    copies = [
-        pltpu.make_async_copy(srcs[0].at[pl.ds(4 * n, 4)], dsts[0].at[pl.ds(4 * n, 4)], sems.at[n])
-        for n in range(4)
-    ]
-    copies += [
-        pltpu.make_async_copy(srcs[n], dsts[n], sems.at[3 + n]) for n in range(1, 8)
-    ]
-    for copy in copies:
-        copy.start()
-    for copy in copies:
-        copy.wait()
+    srcs, dsts, held, arrive, leave = refs[0:8], refs[8:16], refs[16:24], refs[24], refs[25]
+    parts = [tuple(r[0].at[pl.ds(4 * n, 4)] for r in (srcs, held, dsts)) for n in range(4)]
+    parts += [(srcs[n], held[n], dsts[n]) for n in range(1, 8)]
+    fetches = [pltpu.make_async_copy(p[0], p[1], arrive.at[n]) for n, p in enumerate(parts)]
+    stores = [pltpu.make_async_copy(p[1], p[2], leave.at[n]) for n, p in enumerate(parts)]
+    for fetch in fetches:
+        fetch.start()
+    for fetch, store in zip(fetches, stores):
+        fetch.wait()
+        store.start()
+    for store in stores:
+        store.wait()
 
 
 def per_device(
@@ -593,7 +593,8 @@
         out_shape=tuple(shape(out.shape, out.dtype) for out in outs),
         in_specs=[anywhere] * 8,
         out_specs=[anywhere] * 8,
-        scratch_shapes=[pltpu.SemaphoreType.DMA((11,))],
+        scratch_shapes=[pltpu.VMEM(out.shape, out.dtype) for out in outs]
+        + [pltpu.SemaphoreType.DMA((11,))] * 2,
         name="results",
     )(*outs)
     return (

time: 172 us -> 76.6 us (0.45)
  Pallas kernels: 171 us -> 75.6 us
    pallas_call x1, Pallas kernels: 98.6 us -> 2.92 us  [per_device(): pl.pallas_call(finish, out_shape=tuple((shape(out.shape, out.dtype) for o...]
where the time goes in v3:
time: 76.6 us; the launch traced here: 76.4 us
  Pallas kernels  75.6 us (99%)
  between operations  0.82 us (1%)
    pallas_call x1, Pallas kernels, per_device(): pl.pallas_call(kernel, out_shape=(shape((16, 512, 128), BF16), shape((102...  72.7 us
    pallas_call x1, Pallas kernels, per_device(): pl.pallas_call(finish, out_shape=tuple((shape(out.shape, out.dtype) for o...  2.92 us

profile of v3, /device:TPU:1, one launch (start us, length us, event | category | flops | bytes accessed | tf_op | source)
XLA Modules:
  0.0 76.4 jit_solution(11355405757856668244)
XLA Ops:
  0.6 72.7 %outer_product_mean.1 = (bf16[16,512,128]{2,1,0:T(8,128)(2,1)}, bf16[1024,256]{1,0:T(8,128)(2,1)}, f32[64,256]{1,0:T(8,128)}, f32[1,64]{1,0:T(1,128)}, f32[1024,...) custom-call(bf16[1024,256]{1,0:T(8,128)(2,1)} %bitcast.12, s32[64,512]{1,0:T(8,128)} %mask.1, ...), custom_call_target="tpu_custom_call" | custom-call | flops 16000000000 | bytes 6000000 | tf_op jit(solution)/shard_map/outer_product_mean/pallas_call | solution.py:558
  73.3 2.9 %results.1 = (bf16[16,512,128]{2,1,0:T(8,128)(2,1)}, bf16[1024,256]{1,0:T(8,128)(2,1)}, f32[64,256]{1,0:T(8,128)}, f32[1,64]{1,0:T(1,128)}, f32[1024,128]{1,0:T(...) custom-call(bf16[16,512,128]{2,1,0:T(8,128)(2,1)} %get-tuple-element.24.refs_0_, ...), custom_call_target="tpu_custom_call" | custom-call | tf_op jit(solution)/shard_map/results/pallas_call | solution.py:591

commit v4 on v2

--- a/solution.py
+++ b/solution.py
@@ -27,9 +27,9 @@
 
 
 def kernel(
-    al, mask, cot, scales, shifts, proj, offs, readout, biases,
-    pair_o, al_o, pg_o, og_o, rg_o, bg_o, sg_o, hg_o,
-    cot_v, pair_v, al_v, mcol, std, inv, normed, both, l_out, l_in, l_f, l_all, l_t, w, ro_f,
+    al_h, mask_h, cot, scales, shifts, proj, offs, readout_h, biases,
+    pair_v, al_v, pg_o, og_o, rg_o, bg_o, sg_o, hg_o,
+    al, mask, readout, cot_v, mcol, std, inv, normed, both, l_out, l_in, l_f, l_all, l_t, w, ro_f,
     rec, g, perm, perm_t, r_buf, r_k, r_j, t, q,
     d_buf, c_in, s1, x_in, s2, z_in,
     lg_f, lg_out, lg_in, rg_l, rg_f, rg_b, ra, rb, rc, re, rh, rk,
@@ -72,8 +72,13 @@
         return carry
 
     lax.fori_loop(1, 32, greet, 0)
-    cot_copy = pltpu.make_async_copy(cot, cot_v, io.at[0])
-    cot_copy.start()
+    al_copy = pltpu.make_async_copy(al_h, al, io.at[0])
+    mask_copy = pltpu.make_async_copy(mask_h, mask, io.at[1])
+    readout_copy = pltpu.make_async_copy(readout_h, readout, io.at[2])
+    cot_copy = pltpu.make_async_copy(cot, cot_v, io.at[3])
+    for copy in (mask_copy, al_copy, cot_copy, readout_copy):
+        copy.start()
+    mask_copy.wait()
 
     mask_f = mask[...].astype(F32)
     mask_t = mask_f.T
@@ -81,6 +86,7 @@
         mcol[k * 512:(k + 1) * 512, :] = jnp.sum(
             jnp.where(iota((512, 64), 1) == 2 * me + k, mask_t, 0.0), axis=1, keepdims=True
         )
+    al_copy.wait()
     for k in range(2):
         rows = slice(k * 512, (k + 1) * 512)
         wide = al[rows, :].astype(F32)
@@ -135,6 +141,7 @@
         total = total + jnp.sum(sg.astype(F32), axis=0, keepdims=True)
     bsum[...] = total
 
+    readout_copy.wait()
     ro_f[...] = readout[...].astype(F32)
     for d in range(32):
         w[:, d * 128:(d + 1) * 128] = ro_f[pl.ds(d, 32, stride=32), :].astype(BF16)
@@ -227,9 +234,6 @@
     r_send(slot(xf, core, zz), sib, 27)
     t_group(xx)
     d_group(xx, 3)
-    for n, z_ in enumerate((zm, zs, zf)):
-        r_wait(slot(xf, core, z_))
-        r_send(slot(xf, core, z_), sib, 28 + n)
 
     def r_prep(x_):
         for z_ in range(4):
@@ -242,11 +246,13 @@
     def e_copy(s, k):
         return remote(lg_out.at[s], lg_in.at[me], e_ss.at[k], e_rs.at[me], slot_dev(s))
 
-    def q_group(x_, n):
+    def q_group(x_):
         for h in range(2):
             block = mm(r_k[...], g[:, h * 1024:(h + 1) * 1024]).astype(BF16)
             for i in range(8):
                 q[x_, h * 8 + i] = block[:, i * 128:(i + 1) * 128].reshape(32, 16, 128)
+
+    def lg_group(x_, n):
         rows = jnp.concatenate([q[x_, :, d].reshape(256, 128) for d in range(32)], axis=1)
         lg_f[:, 0:32] = mm_nt(rows, w[...])
         for c in range(8):
@@ -267,14 +273,29 @@
             s2.at[z_], z_in.at[zz], d_ss.at[6 + k], d_rs.at[7 + zz], dev(z_, xx, core)
         )
 
+    def rg_group(x_, n):
+        cols = l_t[:, pl.ds(pl.multiple_of(x_ * 256, 256), 256)]
+        rows = jnp.concatenate([q[x_, :, d].reshape(256, 128) for d in range(32)], axis=1)
+        part = mm(cols, rows)
+        rg_l[...] = part if n == 0 else rg_l[...] + part
+
     r_prep(xx)
+    q_group(xx)
     c_wait(xs, 2)
     x_copy(xf, 0, xs).wait_recv()
     s1[xs] = (core_sum(xs) + x_in[0].astype(F32)).astype(BF16)
     x_copy(xs, 2, xs).start()
-    q_group(xx, 0)
+    lg_group(xx, 0)
+    for n, z_ in enumerate((zm, zs, zf)):
+        r_wait(slot(xf, core, z_))
+        r_send(slot(xf, core, z_), sib, 28 + n)
+    rg_group(xx, 0)
     r_prep(xm)
-    q_group(xm, 1)
+    q_group(xm)
+    lg_group(xm, 1)
+    rg_group(xm, 1)
+    r_prep(xs)
+    q_group(xs)
     c_wait(xx, 3)
     x_copy(xm, 1, xm).wait_recv()
     x_copy(xs, 2, xs).wait_recv()
@@ -283,25 +304,18 @@
     ).astype(BF16).reshape(4, 64, 512)
     for k in range(1, 4):
         z_copy(k).start()
-    r_prep(xs)
-    q_group(xs, 2)
+    lg_group(xs, 2)
+    rg_group(xs, 2)
     r_prep(xf)
-    q_group(xf, 3)
-
-    rows_q = jnp.concatenate(
-        [q[:, :, d].reshape(1024, 128) for d in range(32)], axis=1
-    )
-    rg_l[...] = mm(l_t[...], rows_q)
+    q_group(xf)
+
+    rg_group(xf, 3)
     for d in range(32):
         rg_f[pl.ds(d, 32, stride=32), :] = rg_l[:, d * 128:(d + 1) * 128]
     rg_b[...] = rg_f[...].astype(BF16).reshape(2, 512, 128)
     a0 = remote(rg_b.at[other], ra, a_ss.at[0], a_rs.at[0], sib)
     a0.start()
-
-    def pair_copy(ib):
-        return pltpu.make_async_copy(
-            pair_v.at[pl.ds(ib * 4, 4)], pair_o.at[pl.ds(ib * 4, 4)], io.at[ib + 1]
-        )
+    lg_group(xf, 3)
 
     def u_step(ib):
         cols = jnp.concatenate(
@@ -312,7 +326,6 @@
             pair_v[4 * ib + ii] = (
                 (acc[:, ii * 128:(ii + 1) * 128] + biases[...]) * rec[4 * ib + ii]
             ).astype(BF16)
-        pair_copy(ib).start()
 
     u_step(0)
     u_step(1)
@@ -397,8 +410,6 @@
         m1 = jnp.mean(h, axis=-1, keepdims=True)
         m2 = jnp.mean(h * standard, axis=-1, keepdims=True)
         al_v[rows, :] = ((h - m1 - standard * m2) * inv[rows, :]).astype(BF16)
-    al_copy = pltpu.make_async_copy(al_v, al_o, io.at[5])
-    al_copy.start()
     u_step(2)
 
     for k in range(1, 4):
@@ -463,9 +474,6 @@
         a_g(k).wait_send()
         b_x(k).wait_send()
         b_z(k).wait_send()
-    for ib in range(4):
-        pair_copy(ib).wait()
-    al_copy.wait()
     a_last.wait()
     rg_o[pl.ds(pl.multiple_of(other * 512, 512), 512), :] = rk[...].reshape(512, 128).astype(F32)
     remote(
@@ -486,9 +494,7 @@
         pltpu.make_async_copy(srcs[0].at[pl.ds(4 * n, 4)], dsts[0].at[pl.ds(4 * n, 4)], sems.at[n])
         for n in range(4)
     ]
-    copies += [
-        pltpu.make_async_copy(srcs[n], dsts[n], sems.at[3 + n]) for n in range(1, 8)
-    ]
+    copies += [pltpu.make_async_copy(srcs[n], dsts[n], sems.at[3 + n]) for n in range(1, 8)]
     for copy in copies:
         copy.start()
     for copy in copies:
@@ -501,9 +507,10 @@
     vmem = pl.BlockSpec(memory_space=pltpu.VMEM)
     shape = jax.ShapeDtypeStruct
     sizes = dict(
+        al=((1024, 256), BF16),
+        mask=((64, 512), jnp.int32),
+        readout=((1024, 128), BF16),
         cot_v=((16, 512, 128), BF16),
-        pair_v=((16, 512, 128), BF16),
-        al_v=((1024, 256), BF16),
         mcol=((1024, 1), F32),
         std=((1024, 256), F32),
         inv=((1024, 1), F32),
@@ -552,26 +559,26 @@
         bsum=((1, 128), F32),
     )
     scratch = [pltpu.VMEM(*size) for size in sizes.values()] + [
-        pltpu.SemaphoreType.DMA((n,)) for n in (32, 32, 32, 32, 31, 32, 10, 11, 11, 14, 8, 10, 6)
+        pltpu.SemaphoreType.DMA((n,)) for n in (32, 32, 32, 32, 31, 32, 10, 11, 11, 14, 8, 10, 4)
     ]
     anywhere = pl.BlockSpec(memory_space=pl.ANY)
     outs = pl.pallas_call(
         kernel,
         out_shape=(
-            shape((16, 512, 128), BF16),
-            shape((1024, 256), BF16),
-            shape((64, 256), F32),
-            shape((1, 64), F32),
-            shape((1024, 128), F32),
-            shape((1, 128), F32),
-            shape((1, 256), F32),
-            shape((1, 256), F32),
+            pltpu.VMEM((16, 512, 128), BF16),
+            pltpu.VMEM((1024, 256), BF16),
+            pltpu.VMEM((64, 256), F32),
+            pltpu.VMEM((1, 64), F32),
+            pltpu.VMEM((1024, 128), F32),
+            pltpu.VMEM((1, 128), F32),
+            pltpu.VMEM((1, 256), F32),
+            pltpu.VMEM((1, 256), F32),
         ),
-        in_specs=[vmem] * 2 + [anywhere] + [vmem] * 6,
-        out_specs=[anywhere] * 2 + [vmem] * 6,
+        in_specs=[anywhere] * 3 + [vmem] * 4 + [anywhere, vmem],
+        out_specs=[vmem] * 8,
         scratch_shapes=scratch,
         compiler_params=pltpu.CompilerParams(
-            collective_id=0, has_side_effects=True, vmem_limit_bytes=62 * 1024 * 1024
+            collective_id=0, has_side_effects=True, vmem_limit_bytes=56 * 1024 * 1024
         ),
         cost_estimate=pl.CostEstimate(
             flops=16_000_000_000, bytes_accessed=6_000_000, transcendentals=0
@@ -591,11 +598,11 @@
     outs = pl.pallas_call(
         finish,
         out_shape=tuple(shape(out.shape, out.dtype) for out in outs),
-        in_specs=[anywhere] * 8,
+        in_specs=[vmem] * 8,
         out_specs=[anywhere] * 8,
         scratch_shapes=[pltpu.SemaphoreType.DMA((11,))],
         name="results",
-    )(*outs)
+    )(*[pltpu.with_memory_space_constraint(out, pltpu.VMEM) for out in outs])
     return (
         outs[0],
         outs[1].reshape(2, 512, 256),

time: 172 us -> 73.1 us (0.42)
  Pallas kernels: 171 us -> 72.1 us
    pallas_call x1, Pallas kernels: 98.6 us -> 1.79 us  [per_device(): pl.pallas_call(finish, out_shape=tuple((shape(out.shape, out.dtype) for o...]
    pallas_call x1, Pallas kernels: 72.7 us -> 70.3 us  [per_device(): pl.pallas_call(kernel, out_shape=(pltpu.VMEM((16, 512, 128), BF16), pltpu...]
where the time goes in v4:
time: 73.1 us; the launch traced here: 72.9 us
  Pallas kernels  72.1 us (99%)
  between operations  0.82 us (1%)
    pallas_call x1, Pallas kernels, per_device(): pl.pallas_call(kernel, out_shape=(pltpu.VMEM((16, 512, 128), BF16), pltpu...  70.3 us
    pallas_call x1, Pallas kernels, per_device(): pl.pallas_call(finish, out_shape=tuple((shape(out.shape, out.dtype) for o...  1.79 us

profile of v4, /device:TPU:1, one launch (start us, length us, event | category | flops | bytes accessed | tf_op | source)
XLA Modules:
  0.0 72.9 jit_solution(216264402857937891)
XLA Ops:
  0.6 70.3 %outer_product_mean.1 = (bf16[16,512,128]{2,1,0:T(8,128)(2,1)S(1)}, bf16[1024,256]{1,0:T(8,128)(2,1)S(1)}, f32[64,256]{1,0:T(8,128)S(1)}, f32[1,64]{1,0:T(1,128)...) custom-call(bf16[1024,256]{1,0:T(8,128)(2,1)} %bitcast.12, ...), custom_call_target="tpu_custom_call" | custom-call | flops 16000000000 | bytes 6000000 | tf_op jit(solution)/shard_map/outer_product_mean/pallas_call | solution.py:565
  70.9 1.8 %results.1 = (bf16[16,512,128]{2,1,0:T(8,128)(2,1)}, bf16[1024,256]{1,0:T(8,128)(2,1)}, f32[64,256]{1,0:T(8,128)}, f32[1,64]{1,0:T(1,128)}, f32[1024,128]{1,0:T(...) custom-call(bf16[16,512,128]{2,1,0:T(8,128)(2,1)S(1)} %get-tuple-element.24.refs_0_, ...), custom_call_target="tpu_custom_call" | custom-call | tf_op jit(solution)/shard_map/results/pallas_call | solution.py:598

commit v5 on v4

--- a/solution.py
+++ b/solution.py
@@ -27,9 +27,9 @@
 
 
 def kernel(
-    al_h, mask_h, cot, scales, shifts, proj, offs, readout_h, biases,
+    al_h, mask_h, cot, scales_h, shifts_h, proj_h, offs_h, readout_h, biases_h,
     pair_v, al_v, pg_o, og_o, rg_o, bg_o, sg_o, hg_o,
-    al, mask, readout, cot_v, mcol, std, inv, normed, both, l_out, l_in, l_f, l_all, l_t, w, ro_f,
+    al, mask, readout, scales, shifts, proj, offs, biases, cot_v, mcol, std, inv, normed, both, l_out, l_in, l_f, l_all, l_t, w, ro_f,
     rec, g, perm, perm_t, r_buf, r_k, r_j, t, q,
     d_buf, c_in, s1, x_in, s2, z_in,
     lg_f, lg_out, lg_in, rg_l, rg_f, rg_b, ra, rb, rc, re, rh, rk,
@@ -72,13 +72,16 @@
         return carry
 
     lax.fori_loop(1, 32, greet, 0)
-    al_copy = pltpu.make_async_copy(al_h, al, io.at[0])
-    mask_copy = pltpu.make_async_copy(mask_h, mask, io.at[1])
-    readout_copy = pltpu.make_async_copy(readout_h, readout, io.at[2])
-    cot_copy = pltpu.make_async_copy(cot, cot_v, io.at[3])
-    for copy in (mask_copy, al_copy, cot_copy, readout_copy):
-        copy.start()
-    mask_copy.wait()
+    fetches = [
+        pltpu.make_async_copy(src, dst, io.at[n])
+        for n, (src, dst) in enumerate((
+            (mask_h, mask), (al_h, al), (scales_h, scales), (shifts_h, shifts), (proj_h, proj),
+            (offs_h, offs), (cot, cot_v), (readout_h, readout), (biases_h, biases),
+        ))
+    ]
+    for fetch in fetches:
+        fetch.start()
+    fetches[0].wait()
 
     mask_f = mask[...].astype(F32)
     mask_t = mask_f.T
@@ -86,7 +89,8 @@
         mcol[k * 512:(k + 1) * 512, :] = jnp.sum(
             jnp.where(iota((512, 64), 1) == 2 * me + k, mask_t, 0.0), axis=1, keepdims=True
         )
-    al_copy.wait()
+    for fetch in fetches[1:6]:
+        fetch.wait()
     for k in range(2):
         rows = slice(k * 512, (k + 1) * 512)
         wide = al[rows, :].astype(F32)
@@ -106,13 +110,15 @@
 
     pl.semaphore_wait(barrier, 31)
 
-    def l_send(k, carry):
-        s = lax.rem(mine + k, 32)
+    def l_copy(s, k):
         p = slot_dev(s)
-        remote(l_out.at[p], l_in.at[mine], l_ss.at[k], l_rs.at[mine], p).start()
-        return carry
-
-    lax.fori_loop(1, 32, l_send, 0)
+        return remote(l_out.at[p], l_in.at[mine], l_ss.at[k], l_rs.at[mine], p)
+
+    for n, x_ in enumerate((xf, xs, xm)):
+        for k in range(8):
+            l_copy(x_ * 8 + k, n * 8 + k).start()
+    for k in range(1, 8):
+        l_copy(xx * 8 + lax.rem(core * 4 + zz + k, 8), 24 + k).start()
 
     def r_send(s, target, k):
         remote(r_buf.at[s], r_buf.at[s], r_ss.at[k], r_rs.at[s], target).start()
@@ -132,7 +138,7 @@
     mask_own = mm(mask_b, own_cols).astype(BF16)
     recip = 1.0 / (0.001 + mm(mask_t.astype(BF16), mask_own))
     total = jnp.zeros((1, 128), F32)
-    cot_copy.wait()
+    fetches[6].wait()
     for i in range(16):
         rec_i = jnp.broadcast_to(recip[:, i:i + 1], (512, 128))
         rec[i] = rec_i
@@ -141,7 +147,8 @@
         total = total + jnp.sum(sg.astype(F32), axis=0, keepdims=True)
     bsum[...] = total
 
-    readout_copy.wait()
+    fetches[7].wait()
+    fetches[8].wait()
     ro_f[...] = readout[...].astype(F32)
     for d in range(32):
         w[:, d * 128:(d + 1) * 128] = ro_f[pl.ds(d, 32, stride=32), :].astype(BF16)
@@ -152,24 +159,17 @@
     perm[...] = (iota((512, 512), 1) == packed(iota((512, 512), 0))).astype(F32).astype(BF16)
     perm_t[...] = (iota((512, 512), 0) == packed(iota((512, 512), 1))).astype(F32).astype(BF16)
 
-    def l_wait(k, carry):
-        s = lax.rem(mine + k, 32)
-        remote(l_out.at[0], l_in.at[s], l_ss.at[k], l_rs.at[s], sib).wait_recv()
-        return carry
-
-    lax.fori_loop(1, 32, l_wait, 0)
-    l_f[...] = l_in[...].reshape(512, 128).astype(F32)
-    for i in range(16):
-        v = l_f[pl.ds(i, 32, stride=16), :]
-        for x in range(4):
-            part = v[x * 8:x * 8 + 8, :]
-            l_all[x * 256 + i * 16:x * 256 + (i + 1) * 16, :] = jnp.concatenate(
-                [part[:, 0:32], part[:, 64:96]], axis=0
-            ).astype(BF16)
-    l_t[...] = l_all[...].astype(F32).T.astype(BF16)
-
-    def t_group(x_):
-        r = mm(l_all[pl.ds(pl.multiple_of(x_ * 256, 256), 256), :], w[...]).astype(BF16)
+    def t_group(x_, own=False):
+        for k in range(1 if own else 0, 8):
+            s = x_ * 8 + (lax.rem(core * 4 + zz + k, 8) if own else k)
+            remote(l_out.at[0], l_in.at[s], l_ss.at[0], l_rs.at[s], sib).wait_recv()
+        l_f[...] = l_in[pl.ds(x_ * 8, 8)].reshape(128, 128).astype(F32)
+        for i in range(16):
+            part = l_f[pl.ds(i, 8, stride=16), :]
+            l_all[x_, i] = jnp.concatenate([part[:, 0:32], part[:, 64:96]], axis=0).astype(BF16)
+        rows = l_all[x_].reshape(256, 32)
+        l_t[x_] = rows.astype(F32).T.astype(BF16)
+        r = mm(rows, w[...]).astype(BF16)
         for d in range(32):
             t[x_, :, d] = r[:, d * 128:(d + 1) * 128].reshape(16, 16, 128)
 
@@ -190,7 +190,6 @@
             s1.at[x_], x_in.at[n], d_ss.at[4 + n], d_rs.at[4 + n], dev(zz, target_x, core)
         )
 
-    t_group(xf)
     r_wait(slot(xx, core, zm))
     r_send(slot(xx, core, zm), dev(zs, xx, core), 5)
     for n, z_ in enumerate((zm, zs)):
@@ -199,12 +198,13 @@
         r_send(slot(xx, core, z_), dev(zz, xs, core), 6 + 3 * n)
         r_send(slot(xx, core, z_), dev(zz, xm, core), 7 + 3 * n)
         r_send(slot(xx, core, z_), sib, 8 + 3 * n)
-    d_group(xf, 0)
+    t_group(xf)
     r_wait(slot(xm, core, zz))
     r_send(slot(xm, core, zz), dev(zz, xs, core), 15)
     r_send(slot(xm, core, zz), sib, 16)
     r_wait(slot(xs, core, zz))
     r_send(slot(xs, core, zz), sib, 17)
+    d_group(xf, 0)
     t_group(xm)
     r_wait(slot(xx, core, zf))
     r_send(slot(xx, core, zf), dev(zz, xs, core), 12)
@@ -225,14 +225,14 @@
     c_wait(xm, 1)
     s1[xm] = core_sum(xm).astype(BF16)
     x_copy(xm, 1, xm).start()
+    r_wait(slot(xf, core, zz))
+    r_send(slot(xf, core, zz), sib, 27)
+    t_group(xx, own=True)
     r_wait(slot(xm, core, zf))
     r_send(slot(xm, core, zf), dev(zz, xs, core), 24)
     r_send(slot(xm, core, zf), sib, 25)
     r_wait(slot(xs, core, zf))
     r_send(slot(xs, core, zf), sib, 26)
-    r_wait(slot(xf, core, zz))
-    r_send(slot(xf, core, zz), sib, 27)
-    t_group(xx)
     d_group(xx, 3)
 
     def r_prep(x_):
@@ -274,9 +274,8 @@
         )
 
     def rg_group(x_, n):
-        cols = l_t[:, pl.ds(pl.multiple_of(x_ * 256, 256), 256)]
         rows = jnp.concatenate([q[x_, :, d].reshape(256, 128) for d in range(32)], axis=1)
-        part = mm(cols, rows)
+        part = mm(l_t[x_], rows)
         rg_l[...] = part if n == 0 else rg_l[...] + part
 
     r_prep(xx)
@@ -285,11 +284,13 @@
     x_copy(xf, 0, xs).wait_recv()
     s1[xs] = (core_sum(xs) + x_in[0].astype(F32)).astype(BF16)
     x_copy(xs, 2, xs).start()
-    lg_group(xx, 0)
-    for n, z_ in enumerate((zm, zs, zf)):
+    for n, z_ in enumerate((zm, zs)):
         r_wait(slot(xf, core, z_))
         r_send(slot(xf, core, z_), sib, 28 + n)
+    lg_group(xx, 0)
     rg_group(xx, 0)
+    r_wait(slot(xf, core, zf))
+    r_send(slot(xf, core, zf), sib, 30)
     r_prep(xm)
     q_group(xm)
     lg_group(xm, 1)
@@ -328,8 +329,6 @@
             ).astype(BF16)
 
     u_step(0)
-    u_step(1)
-
     a0.wait_recv()
     rb[...] = (rg_b[core].astype(F32) + ra[...].astype(F32)).astype(BF16).reshape(4, 128, 128)
 
@@ -340,6 +339,7 @@
     for k in range(1, 4):
         a_x(k).start()
     rc[xx] = rb[xx]
+    u_step(1)
 
     for k in range(1, 32):
         p = lax.rem(me + k, 32)
@@ -454,12 +454,14 @@
     b_last.start()
 
     def drain(k, carry):
-        remote(l_out.at[0], l_in.at[0], l_ss.at[k], l_rs.at[0], sib).wait_send()
         remote(lg_out.at[0], lg_in.at[0], e_ss.at[k], e_rs.at[0], sib).wait_send()
         remote(r_buf.at[0], r_buf.at[0], r_ss.at[k - 1], r_rs.at[0], sib).wait_send()
         return carry
 
     lax.fori_loop(1, 32, drain, 0)
+    for k in range(32):
+        if k != 24:
+            remote(l_out.at[0], l_in.at[0], l_ss.at[k], l_rs.at[0], sib).wait_send()
     for n, x_ in enumerate((xf, xm, xs, xx)):
         remote(d_buf.at[x_, other], c_in.at[x_], d_ss.at[n], d_rs.at[x_], sib).wait_send()
     x_copy(xf, 0, xs).wait_send()
@@ -510,6 +512,11 @@
         al=((1024, 256), BF16),
         mask=((64, 512), jnp.int32),
         readout=((1024, 128), BF16),
+        scales=((1, 256), F32),
+        shifts=((1, 256), F32),
+        proj=((64, 256), BF16),
+        offs=((1, 64), F32),
+        biases=((1, 128), F32),
         cot_v=((16, 512, 128), BF16),
         mcol=((1024, 1), F32),
         std=((1024, 256), F32),
@@ -518,9 +525,9 @@
         both=((1024, 64), F32),
         l_out=((32, 16, 128), BF16),
         l_in=((32, 16, 128), BF16),
-        l_f=((512, 128), F32),
-        l_all=((1024, 32), BF16),
-        l_t=((32, 1024), BF16),
+        l_f=((128, 128), F32),
+        l_all=((4, 16, 16, 32), BF16),
+        l_t=((4, 32, 256), BF16),
         w=((32, 4096), BF16),
         ro_f=((1024, 128), F32),
         rec=((16, 512, 128), F32),
@@ -559,7 +566,7 @@
         bsum=((1, 128), F32),
     )
     scratch = [pltpu.VMEM(*size) for size in sizes.values()] + [
-        pltpu.SemaphoreType.DMA((n,)) for n in (32, 32, 32, 32, 31, 32, 10, 11, 11, 14, 8, 10, 4)
+        pltpu.SemaphoreType.DMA((n,)) for n in (32, 32, 32, 32, 31, 32, 10, 11, 11, 14, 8, 10, 9)
     ]
     anywhere = pl.BlockSpec(memory_space=pl.ANY)
     outs = pl.pallas_call(
@@ -574,7 +581,7 @@
             pltpu.VMEM((1, 256), F32),
             pltpu.VMEM((1, 256), F32),
         ),
-        in_specs=[anywhere] * 3 + [vmem] * 4 + [anywhere, vmem],
+        in_specs=[anywhere] * 9,
         out_specs=[vmem] * 8,
         scratch_shapes=scratch,
         compiler_params=pltpu.CompilerParams(

time: 73.1 us -> 71.3 us (0.975)
  Pallas kernels: 72.1 us -> 70.4 us
    pallas_call x1, Pallas kernels: 70.3 us -> 68.6 us  [per_device(): pl.pallas_call(kernel, out_shape=(pltpu.VMEM((16, 512, 128), BF16), pltpu...]
where the time goes in v5:
time: 71.3 us; the launch traced here: 71.2 us
  Pallas kernels  70.4 us (99%)
  between operations  0.8 us (1%)
    pallas_call x1, Pallas kernels, per_device(): pl.pallas_call(kernel, out_shape=(pltpu.VMEM((16, 512, 128), BF16), pltpu...  68.6 us
    pallas_call x1, Pallas kernels, per_device(): pl.pallas_call(finish, out_shape=tuple((shape(out.shape, out.dtype) for o...  1.79 us

profile of v5, /device:TPU:1, one launch (start us, length us, event | category | flops | bytes accessed | tf_op | source)
XLA Modules:
  0.0 71.2 jit_solution(15757909963812478357)
XLA Ops:
  0.6 68.6 %outer_product_mean.1 = (bf16[16,512,128]{2,1,0:T(8,128)(2,1)S(1)}, bf16[1024,256]{1,0:T(8,128)(2,1)S(1)}, f32[64,256]{1,0:T(8,128)S(1)}, f32[1,64]{1,0:T(1,128)...) custom-call(bf16[1024,256]{1,0:T(8,128)(2,1)} %bitcast.12, ...), custom_call_target="tpu_custom_call" | custom-call | flops 16000000000 | bytes 6000000 | tf_op jit(solution)/shard_map/outer_product_mean/pallas_call | solution.py:572
  69.3 1.8 %results.1 = (bf16[16,512,128]{2,1,0:T(8,128)(2,1)}, bf16[1024,256]{1,0:T(8,128)(2,1)}, f32[64,256]{1,0:T(8,128)}, f32[1,64]{1,0:T(1,128)}, f32[1024,128]{1,0:T(...) custom-call(bf16[16,512,128]{2,1,0:T(8,128)(2,1)S(1)} %get-tuple-element.24.refs_0_, ...), custom_call_target="tpu_custom_call" | custom-call | tf_op jit(solution)/shard_map/results/pallas_call | solution.py:605

commit v6 on v5

--- a/solution.py
+++ b/solution.py
@@ -29,9 +29,10 @@
 def kernel(
     al_h, mask_h, cot, scales_h, shifts_h, proj_h, offs_h, readout_h, biases_h,
     pair_v, al_v, pg_o, og_o, rg_o, bg_o, sg_o, hg_o,
-    al, mask, readout, scales, shifts, proj, offs, biases, cot_v, mcol, std, inv, normed, both, l_out, l_in, l_f, l_all, l_t, w, ro_f,
+    al, mask, readout, scales, shifts, proj, offs, biases, cot_v,
+    mcol, std, inv, normed, both, l_out, l_in, l_f, l_all, l_t, w, ro_f,
     rec, g, perm, perm_t, r_buf, r_k, r_j, t, q,
-    d_buf, c_in, s1, x_in, s2, z_in,
+    d_buf, c_in, s1, x_in, s2, z_in, right_out, right_in,
     lg_f, lg_out, lg_in, rg_l, rg_f, rg_b, ra, rb, rc, re, rh, rk,
     ng_s, pb, pb_core, pb_x, pb_z, pb_half, bsum,
     l_ss, l_rs, e_ss, e_rs, r_ss, r_rs, d_ss, d_rs, a_ss, a_rs, b_ss, b_rs, io,
@@ -176,7 +177,8 @@
     def d_group(x_, n):
         rows = jnp.concatenate([t[x_, i].reshape(512, 128) for i in range(16)], axis=1)
         raw = mm_nt(rows, g[...]).astype(BF16)
-        d_buf[x_] = mm(perm_t[...], raw).astype(BF16).reshape(2, 256, 512)
+        for h in range(2):
+            d_buf[x_, h] = raw[:, h * 256:(h + 1) * 256]
         remote(d_buf.at[x_, other], c_in.at[x_], d_ss.at[n], d_rs.at[x_], sib).start()
 
     def c_wait(x_, n):
@@ -300,9 +302,10 @@
     c_wait(xx, 3)
     x_copy(xm, 1, xm).wait_recv()
     x_copy(xs, 2, xs).wait_recv()
-    s2[...] = (
-        core_sum(xx) + x_in[1].astype(F32) + x_in[2].astype(F32)
-    ).astype(BF16).reshape(4, 64, 512)
+    own_sum = (core_sum(xx) + x_in[1].astype(F32) + x_in[2].astype(F32)).astype(BF16)
+    own_rows = mm(perm_t[...], own_sum).astype(BF16).reshape(2, 4, 64, 256)
+    for c in range(2):
+        s2[:, c] = own_rows[c]
     for k in range(1, 4):
         z_copy(k).start()
     lg_group(xs, 2)
@@ -341,17 +344,26 @@
     rc[xx] = rb[xx]
     u_step(1)
 
+    for k in range(1, 4):
+        z_ = lax.rem(zz + k, 4)
+        remote(s2.at[z_], z_in.at[z_], d_ss.at[6 + k], d_rs.at[7 + z_], sib).wait_recv()
+    z_in[zz] = s2[zz]
+    right_out[...] = (
+        (z_in[0].astype(F32) + z_in[1].astype(F32))
+        + (z_in[2].astype(F32) + z_in[3].astype(F32))
+    ).astype(BF16)
+    f_copy = remote(right_out.at[other], right_in.at[core], d_ss.at[10], d_rs.at[11], sib)
+    f_copy.start()
+    right_in[core] = right_out[core]
     for k in range(1, 32):
         p = lax.rem(me + k, 32)
         remote(lg_out.at[0], lg_in.at[p], e_ss.at[k], e_rs.at[p], sib).wait_recv()
-    for k in range(1, 4):
-        z_ = lax.rem(zz + k, 4)
-        remote(s2.at[z_], z_in.at[z_], d_ss.at[6 + k], d_rs.at[7 + z_], sib).wait_recv()
-    z_in[zz] = s2[zz]
-    right = (z_in[0].astype(F32) + z_in[1].astype(F32)) + (
-        z_in[2].astype(F32) + z_in[3].astype(F32)
+    remote(
+        right_out.at[other], right_in.at[other], d_ss.at[10], d_rs.at[11], sib
+    ).wait_recv()
+    right_t = jnp.concatenate(
+        [right_in[0].astype(F32).T, right_in[1].astype(F32).T], axis=0
     )
-    right_t = right.T
     left = lg_in[...].reshape(512, 128).astype(F32)
     for k in range(2):
         both[k * 512:(k + 1) * 512, :] = jnp.concatenate(
@@ -469,6 +481,7 @@
     x_copy(xs, 2, xs).wait_send()
     a0.wait_send()
     b0.wait_send()
+    f_copy.wait_send()
     for k in range(1, 4):
         z_copy(k).wait_send()
         a_x(k).wait_send()
@@ -539,12 +552,14 @@
         r_j=((512, 2048), BF16),
         t=((4, 16, 32, 16, 128), BF16),
         q=((4, 16, 32, 16, 128), BF16),
-        d_buf=((4, 2, 256, 512), BF16),
-        c_in=((4, 256, 512), BF16),
-        s1=((4, 256, 512), BF16),
-        x_in=((3, 256, 512), BF16),
-        s2=((4, 64, 512), BF16),
-        z_in=((4, 64, 512), BF16),
+        d_buf=((4, 2, 512, 256), BF16),
+        c_in=((4, 512, 256), BF16),
+        s1=((4, 512, 256), BF16),
+        x_in=((3, 512, 256), BF16),
+        s2=((4, 2, 64, 256), BF16),
+        z_in=((4, 2, 64, 256), BF16),
+        right_out=((2, 64, 256), BF16),
+        right_in=((2, 64, 256), BF16),
         lg_f=((256, 128), F32),
         lg_out=((32, 16, 128), BF16),
         lg_in=((32, 16, 128), BF16),
@@ -566,7 +581,7 @@
         bsum=((1, 128), F32),
     )
     scratch = [pltpu.VMEM(*size) for size in sizes.values()] + [
-        pltpu.SemaphoreType.DMA((n,)) for n in (32, 32, 32, 32, 31, 32, 10, 11, 11, 14, 8, 10, 9)
+        pltpu.SemaphoreType.DMA((n,)) for n in (32, 32, 32, 32, 31, 32, 11, 12, 11, 14, 8, 10, 9)
     ]
     anywhere = pl.BlockSpec(memory_space=pl.ANY)
     outs = pl.pallas_call(

time: 71.3 us -> 71.6 us (level)
  no operation moved by 1% of the time
where the time goes in v6:
time: 71.6 us; the launch traced here: 71.5 us
  Pallas kernels  70.7 us (99%)
  between operations  0.8 us (1%)
    pallas_call x1, Pallas kernels, per_device(): pl.pallas_call(kernel, out_shape=(pltpu.VMEM((16, 512, 128), BF16), pltpu...  68.9 us
    pallas_call x1, Pallas kernels, per_device(): pl.pallas_call(finish, out_shape=tuple((shape(out.shape, out.dtype) for o...  1.79 us

profile of v6, /device:TPU:1, one launch (start us, length us, event | category | flops | bytes accessed | tf_op | source)
XLA Modules:
  0.0 71.5 jit_solution(908312075936208335)
XLA Ops:
  0.6 68.9 %outer_product_mean.1 = (bf16[16,512,128]{2,1,0:T(8,128)(2,1)S(1)}, bf16[1024,256]{1,0:T(8,128)(2,1)S(1)}, f32[64,256]{1,0:T(8,128)S(1)}, f32[1,64]{1,0:T(1,128)...) custom-call(bf16[1024,256]{1,0:T(8,128)(2,1)} %bitcast.12, ...), custom_call_target="tpu_custom_call" | custom-call | flops 16000000000 | bytes 6000000 | tf_op jit(solution)/shard_map/outer_product_mean/pallas_call | solution.py:587
  69.6 1.8 %results.1 = (bf16[16,512,128]{2,1,0:T(8,128)(2,1)}, bf16[1024,256]{1,0:T(8,128)(2,1)}, f32[64,256]{1,0:T(8,128)}, f32[1,64]{1,0:T(1,128)}, f32[1024,128]{1,0:T(...) custom-call(bf16[16,512,128]{2,1,0:T(8,128)(2,1)S(1)} %get-tuple-element.24.refs_0_, ...), custom_call_target="tpu_custom_call" | custom-call | tf_op jit(solution)/shard_map/results/pallas_call | solution.py:620

commit v7 on v6

--- a/solution.py
+++ b/solution.py
@@ -115,23 +115,24 @@
         p = slot_dev(s)
         return remote(l_out.at[p], l_in.at[mine], l_ss.at[k], l_rs.at[mine], p)
 
-    for n, x_ in enumerate((xf, xs, xm)):
-        for k in range(8):
-            l_copy(x_ * 8 + k, n * 8 + k).start()
-    for k in range(1, 8):
-        l_copy(xx * 8 + lax.rem(core * 4 + zz + k, 8), 24 + k).start()
-
     def r_send(s, target, k):
         remote(r_buf.at[s], r_buf.at[s], r_ss.at[k], r_rs.at[s], target).start()
 
     def r_wait(s):
         remote(r_buf.at[s], r_buf.at[s], r_ss.at[0], r_rs.at[s], sib).wait_recv()
 
+    for k in range(8):
+        l_copy(xf * 8 + k, k).start()
     r_send(mine, dev(zs, xx, core), 0)
     r_send(mine, dev(zm, xx, core), 1)
     r_send(mine, dev(zz, xs, core), 2)
     r_send(mine, dev(zz, xm, core), 3)
     r_send(mine, sib, 4)
+    for n, x_ in ((1, xs), (2, xm)):
+        for k in range(8):
+            l_copy(x_ * 8 + k, n * 8 + k).start()
+    for k in range(1, 8):
+        l_copy(xx * 8 + lax.rem(core * 4 + zz + k, 8), 24 + k).start()
     l_in[mine] = l_out[me]
 
     mask_b = mask_f.astype(BF16)
@@ -451,20 +452,6 @@
         b_z(k).start()
     u_step(3)
 
-    for k in range(1, 4):
-        x_ = lax.rem(xx + k, 4)
-        remote(rh.at[x_], rh.at[x_], a_ss.at[6 + k], a_rs.at[9 + x_], sib).wait_recv()
-    a_last = remote(rh, rk, a_ss.at[10], a_rs.at[13], sib)
-    a_last.start()
-    rg_o[pl.ds(pl.multiple_of(core * 512, 512), 512), :] = rh[...].reshape(512, 128).astype(F32)
-
-    for k in range(1, 4):
-        z_ = lax.rem(zz + k, 4)
-        remote(pb_z.at[z_], pb_z.at[z_], b_ss.at[3 + k], b_rs.at[5 + z_], sib).wait_recv()
-    pb_half[core] = four(pb_z).astype(BF16)
-    b_last = remote(pb_half.at[core], pb_half.at[core], b_ss.at[7], b_rs.at[9], sib)
-    b_last.start()
-
     def drain(k, carry):
         remote(lg_out.at[0], lg_in.at[0], e_ss.at[k], e_rs.at[0], sib).wait_send()
         remote(r_buf.at[0], r_buf.at[0], r_ss.at[k - 1], r_rs.at[0], sib).wait_send()
@@ -479,15 +466,30 @@
     x_copy(xf, 0, xs).wait_send()
     x_copy(xm, 1, xm).wait_send()
     x_copy(xs, 2, xs).wait_send()
+    for k in range(1, 4):
+        z_copy(k).wait_send()
+        a_x(k).wait_send()
+        a_z(k).wait_send()
+        b_x(k).wait_send()
     a0.wait_send()
     b0.wait_send()
     f_copy.wait_send()
-    for k in range(1, 4):
-        z_copy(k).wait_send()
-        a_x(k).wait_send()
-        a_z(k).wait_send()
+
+    for k in range(1, 4):
+        x_ = lax.rem(xx + k, 4)
+        remote(rh.at[x_], rh.at[x_], a_ss.at[6 + k], a_rs.at[9 + x_], sib).wait_recv()
+    a_last = remote(rh, rk, a_ss.at[10], a_rs.at[13], sib)
+    a_last.start()
+    rg_o[pl.ds(pl.multiple_of(core * 512, 512), 512), :] = rh[...].reshape(512, 128).astype(F32)
+
+    for k in range(1, 4):
+        z_ = lax.rem(zz + k, 4)
+        remote(pb_z.at[z_], pb_z.at[z_], b_ss.at[3 + k], b_rs.at[5 + z_], sib).wait_recv()
+    pb_half[core] = four(pb_z).astype(BF16)
+    b_last = remote(pb_half.at[core], pb_half.at[core], b_ss.at[7], b_rs.at[9], sib)
+    b_last.start()
+    for k in range(1, 4):
         a_g(k).wait_send()
-        b_x(k).wait_send()
         b_z(k).wait_send()
     a_last.wait()
     rg_o[pl.ds(pl.multiple_of(other * 512, 512), 512), :] = rk[...].reshape(512, 128).astype(F32)

time: 71.6 us -> 70 us (0.978)
  Pallas kernels: 70.7 us -> 69 us
    pallas_call x1, Pallas kernels: 68.9 us -> 67.3 us  [per_device(): pl.pallas_call(kernel, out_shape=(pltpu.VMEM((16, 512, 128), BF16), pltpu...]
where the time goes in v7:
time: 70 us; the launch traced here: 69.9 us
  Pallas kernels  69 us (99%)
  between operations  0.8 us (1%)
    pallas_call x1, Pallas kernels, per_device(): pl.pallas_call(kernel, out_shape=(pltpu.VMEM((16, 512, 128), BF16), pltpu...  67.3 us
    pallas_call x1, Pallas kernels, per_device(): pl.pallas_call(finish, out_shape=tuple((shape(out.shape, out.dtype) for o...  1.79 us

profile of v7, /device:TPU:1, one launch (start us, length us, event | category | flops | bytes accessed | tf_op | source)
XLA Modules:
  0.0 69.9 jit_solution(8113086112194017113)
XLA Ops:
  0.6 67.3 %outer_product_mean.1 = (bf16[16,512,128]{2,1,0:T(8,128)(2,1)S(1)}, bf16[1024,256]{1,0:T(8,128)(2,1)S(1)}, f32[64,256]{1,0:T(8,128)S(1)}, f32[1,64]{1,0:T(1,128)...) custom-call(bf16[1024,256]{1,0:T(8,128)(2,1)} %bitcast.12, ...), custom_call_target="tpu_custom_call" | custom-call | flops 16000000000 | bytes 6000000 | tf_op jit(solution)/shard_map/outer_product_mean/pallas_call | solution.py:589
  67.9 1.8 %results.1 = (bf16[16,512,128]{2,1,0:T(8,128)(2,1)}, bf16[1024,256]{1,0:T(8,128)(2,1)}, f32[64,256]{1,0:T(8,128)}, f32[1,64]{1,0:T(1,128)}, f32[1024,128]{1,0:T(...) custom-call(bf16[16,512,128]{2,1,0:T(8,128)(2,1)S(1)} %get-tuple-element.24.refs_0_, ...), custom_call_target="tpu_custom_call" | custom-call | tf_op jit(solution)/shard_map/results/pallas_call | solution.py:622

commit v8 on v7

--- a/solution.py
+++ b/solution.py
@@ -121,10 +121,10 @@
     def r_wait(s):
         remote(r_buf.at[s], r_buf.at[s], r_ss.at[0], r_rs.at[s], sib).wait_recv()
 
+    r_send(mine, dev(zs, xx, core), 0)
+    r_send(mine, dev(zm, xx, core), 1)
     for k in range(8):
         l_copy(xf * 8 + k, k).start()
-    r_send(mine, dev(zs, xx, core), 0)
-    r_send(mine, dev(zm, xx, core), 1)
     r_send(mine, dev(zz, xs, core), 2)
     r_send(mine, dev(zz, xm, core), 3)
     r_send(mine, sib, 4)

time: 70 us -> 69.6 us (level)
  no operation moved by 1% of the time
where the time goes in v8:
time: 69.6 us; the launch traced here: 69.5 us
  Pallas kernels  68.6 us (99%)
  between operations  0.8 us (1%)
    pallas_call x1, Pallas kernels, per_device(): pl.pallas_call(kernel, out_shape=(pltpu.VMEM((16, 512, 128), BF16), pltpu...  66.9 us
    pallas_call x1, Pallas kernels, per_device(): pl.pallas_call(finish, out_shape=tuple((shape(out.shape, out.dtype) for o...  1.79 us

profile of v8, /device:TPU:1, one launch (start us, length us, event | category | flops | bytes accessed | tf_op | source)
XLA Modules:
  0.0 69.5 jit_solution(2480944119322436057)
XLA Ops:
  0.6 66.9 %outer_product_mean.1 = (bf16[16,512,128]{2,1,0:T(8,128)(2,1)S(1)}, bf16[1024,256]{1,0:T(8,128)(2,1)S(1)}, f32[64,256]{1,0:T(8,128)S(1)}, f32[1,64]{1,0:T(1,128)...) custom-call(bf16[1024,256]{1,0:T(8,128)(2,1)} %bitcast.12, ...), custom_call_target="tpu_custom_call" | custom-call | flops 16000000000 | bytes 6000000 | tf_op jit(solution)/shard_map/outer_product_mean/pallas_call | solution.py:589
  67.5 1.8 %results.1 = (bf16[16,512,128]{2,1,0:T(8,128)(2,1)}, bf16[1024,256]{1,0:T(8,128)(2,1)}, f32[64,256]{1,0:T(8,128)}, f32[1,64]{1,0:T(1,128)}, f32[1024,128]{1,0:T(...) custom-call(bf16[16,512,128]{2,1,0:T(8,128)(2,1)S(1)} %get-tuple-element.24.refs_0_, ...), custom_call_target="tpu_custom_call" | custom-call | tf_op jit(solution)/shard_map/results/pallas_call | solution.py:622
